TPU v7x, 256 devices: a whole 4x4x8 slice. The times are simulated.
256 devices in a mesh: gx: 16 (over x_lo, y, core), gy: 16 (over z, x_hi).
Axes of the slice: x: 4 (x_hi: 2, x_lo: 2; x = x_hi * 2 + x_lo), y: 4, z: 8, core: 2. Of those that a mesh axis runs over, the one named last changes fastest.
Arguments:
- offsets: float32 [3, 32, 32, 4, 128], P(None, 'gx', 'gy'), may hold values from 0 to 1
- charges: float32 [32, 32, 4, 128], P('gx', 'gy'), may hold values from -0.12 to 0.12
- counts: int32 [32, 32, 4], P('gx', 'gy'), may hold values from 16 to 128, as said below
- c2e_leaf_up: float32 [256, 256], replicated, may hold values from -0.09375 to 0.09375
- c2e_leaf_down: float32 [256, 256], replicated, may hold values from -0.09375 to 0.09375
- c2e_top_up: float32 [256, 256], replicated, may hold values from -0.046875 to 0.046875
- c2e_top_down: float32 [256, 256], replicated, may hold values from -0.046875 to 0.046875
Outputs:
- potential: float32 [32, 32, 4, 128], P('gx', 'gy')
Inputs may be any that keep to these rules, and one draw needn't show every extreme that they name: The first counts slots of a leaf box hold its particles, the rest are padding.
All inputs are finite; a program needn't handle non-finite values.
Results may differ from a plain program's by a relative error of at most 0.0003.
Values sent between devices are 32-bit elements; how exact they have to be, the bound alone decides.
A program may use at most 64 MiB of HBM per device.

v0:
```python
import jax
import jax.numpy as jnp
from jax import lax
from jax.sharding import PartitionSpec as P

softening_sq = 0.0004
golden_turn = 2.399963229728653
highest = lax.Precision.HIGHEST


def padded(cells, sides, width):
    for axis, dim in sides:
        count = lax.axis_size(axis)
        head = lax.slice_in_dim(cells, 0, width, axis=dim)
        tail = lax.slice_in_dim(cells, cells.shape[dim] - width, cells.shape[dim], axis=dim)
        cells = jnp.concatenate(
            [
                lax.ppermute(tail, axis, [(i, (i + 1) % count) for i in range(count)]),
                cells,
                lax.ppermute(head, axis, [((i + 1) % count, i) for i in range(count)]),
            ],
            axis=dim,
        )
    return cells


def sphere(point_count):
    middle = jnp.arange(point_count).astype(jnp.float32) + 0.5
    height = 1.0 - 2.0 * middle / point_count
    radial = jnp.sqrt(jnp.maximum(1.0 - height * height, 0.0))
    angle_turn = middle * golden_turn
    return jnp.stack([radial * jnp.cos(angle_turn), radial * jnp.sin(angle_turn), height])


def point_sum(targets, sources, weights):
    delta_x = targets[0][..., :, None] - sources[0][..., None, :]
    delta_y = targets[1][..., :, None] - sources[1][..., None, :]
    delta_z = targets[2][..., :, None] - sources[2][..., None, :]
    kernel = lax.rsqrt(delta_x * delta_x + delta_y * delta_y + delta_z * delta_z + softening_sq)
    return jnp.sum(kernel * weights[..., None, :], axis=-1)


def translation(unit_sphere, shift_x, shift_y, shift_z, radius):
    delta_x = (
        radius * (unit_sphere[0][:, None] - unit_sphere[0][None, :]) - shift_x[..., None, None]
    )
    delta_y = (
        radius * (unit_sphere[1][:, None] - unit_sphere[1][None, :]) - shift_y[..., None, None]
    )
    delta_z = (
        radius * (unit_sphere[2][:, None] - unit_sphere[2][None, :]) - shift_z[..., None, None]
    )
    return lax.rsqrt(delta_x * delta_x + delta_y * delta_y + delta_z * delta_z + softening_sq)


def child_points(unit_sphere):
    centre = jnp.arange(2).astype(jnp.float32) + 0.5
    point_count = unit_sphere.shape[1]
    box_shape = (2, 2, 2, point_count)
    along_x = jnp.broadcast_to(centre[:, None, None, None] + 0.9 * unit_sphere[0], box_shape)
    along_y = jnp.broadcast_to(centre[None, :, None, None] + 0.9 * unit_sphere[1], box_shape)
    along_z = jnp.broadcast_to(centre[None, None, :, None] + 0.9 * unit_sphere[2], box_shape)
    return jnp.stack([along_x, along_y, along_z]).reshape(3, 8 * point_count)


def shards(offsets, charges, counts, c2e_leaf_up, c2e_leaf_down, c2e_top_up, c2e_top_down):
    slot_count = offsets.shape[-1]
    layers = offsets.shape[3]
    parent_layers = layers // 2
    points = c2e_leaf_up.shape[0]
    unit_sphere = sphere(points)
    slot_index = jnp.arange(slot_count)
    weights = jnp.where(slot_index < counts[..., None], charges, 0.0)
    packed = jnp.concatenate([offsets, weights[None]], axis=0)
    beside_all = padded(packed, (("gx", 1), ("gy", 2)), 1)
    leaf_check_pts = 0.5 + 1.8 * unit_sphere
    leaf_check = point_sum(leaf_check_pts[:, None, None, None, :], offsets, weights)
    leaf_eq = jnp.einsum("ec,xyzc->xyze", c2e_leaf_up, leaf_check, precision=highest)
    children = child_points(unit_sphere)
    parent_weights = (
        leaf_eq.reshape(2, 2, parent_layers, 2, points)
        .transpose(2, 0, 1, 3, 4)
        .reshape(parent_layers, 8 * points)
    )
    parent_check_pts = 1.0 + 3.6 * unit_sphere
    parent_check = point_sum(parent_check_pts[:, None, :], children[:, None, :], parent_weights)
    parent_eq = jnp.einsum("ec,mc->me", c2e_top_up, parent_check, precision=highest)
    count_x = lax.axis_size("gx")
    count_y = lax.axis_size("gy")
    own_x = lax.axis_index("gx")
    own_y = lax.axis_index("gy")
    layer_float = jnp.arange(parent_layers).astype(jnp.float32)
    depth_pairs = 2.0 * (layer_float[None, :] - layer_float[:, None])
    pair_ones = jnp.ones((parent_layers, parent_layers), jnp.float32)
    local_index = jnp.arange(2)
    layer_index = jnp.arange(layers)
    depth_shift = jnp.arange(7) - 3
    depth_float = depth_shift.astype(jnp.float32)
    valid_z = (layer_index[None, :] + depth_shift[:, None] >= 0) & (
        layer_index[None, :] + depth_shift[:, None] <= layers - 1
    )

    def far_term(target_x, target_y, source_x, source_y, density):
        off_x = (source_x - target_x + count_x // 2) % count_x - count_x // 2
        off_y = (source_y - target_y + count_y // 2) % count_y - count_y // 2
        keep = ((jnp.abs(off_x) > 1) | (jnp.abs(off_y) > 1)).astype(jnp.float32)
        matrices = translation(
            unit_sphere,
            2.0 * off_x.astype(jnp.float32) * pair_ones,
            2.0 * off_y.astype(jnp.float32) * pair_ones,
            depth_pairs,
            1.8,
        )
        return keep * jnp.sum(matrices * density[None, :, None, :], axis=(1, 3))

    def neighbour_leaves(off_x, off_y, source_leaves):
        framed_z = jnp.pad(source_leaves, ((0, 0), (0, 0), (3, 3), (0, 0)))
        stacked = jnp.stack([framed_z[:, :, depth : depth + layers] for depth in range(7)], axis=2)
        result = jnp.zeros((2, 2, layers, points), jnp.float32)
        for source_i in range(2):
            for source_j in range(2):
                step_x = 2 * off_x + source_i - local_index
                step_y = 2 * off_y + source_j - local_index
                grid_x = jnp.broadcast_to(step_x[:, None, None], (2, 2, 7))
                grid_y = jnp.broadcast_to(step_y[None, :, None], (2, 2, 7))
                grid_z = jnp.broadcast_to(depth_shift[None, None, :], (2, 2, 7))
                far_enough = (jnp.abs(grid_x) > 1) | (jnp.abs(grid_y) > 1) | (jnp.abs(grid_z) > 1)
                keep = far_enough[..., None] & valid_z[None, None]
                matrices = translation(
                    unit_sphere,
                    grid_x.astype(jnp.float32),
                    grid_y.astype(jnp.float32),
                    jnp.broadcast_to(depth_float[None, None, :], (2, 2, 7)),
                    0.9,
                )
                sources = jnp.where(keep[..., None], stacked[source_i, source_j][None, None], 0.0)
                result = result + jnp.einsum(
                    "ijzce,ijzke->ijkc", matrices, sources, precision=highest
                )
        return result

    start_carry = (
        jnp.zeros((parent_layers, points), jnp.float32),
        jnp.zeros((2, 2, layers, points), jnp.float32),
    )
    leaf_piece = lax.all_gather(leaf_eq[None], ("gx", "gy"), axis=0, tiled=True)
    parent_piece = lax.all_gather(parent_eq[None], ("gx", "gy"), axis=0, tiled=True)

    def one_source(member, carry):
        far_acc, leaf_acc = carry
        source_x = member // count_y
        source_y = member % count_y
        far_acc = far_acc + far_term(own_x, own_y, source_x, source_y, parent_piece[member])
        off_x = (source_x - own_x + count_x // 2) % count_x - count_x // 2
        off_y = (source_y - own_y + count_y // 2) % count_y - count_y // 2
        beside = (jnp.abs(off_x) <= 1) & (jnp.abs(off_y) <= 1)
        source_leaves = leaf_piece[member]
        leaf_acc = lax.cond(
            beside,
            lambda acc: acc + neighbour_leaves(off_x, off_y, source_leaves),
            lambda acc: acc,
            leaf_acc,
        )
        return (far_acc, leaf_acc)

    far_check, leaf_down_check = lax.fori_loop(0, parent_piece.shape[0], one_source, start_carry)
    parent_local = jnp.einsum("ec,mc->me", c2e_top_down, far_check, precision=highest)
    leaf_local = jnp.einsum("ec,xyzc->xyze", c2e_leaf_down, leaf_down_check, precision=highest)
    padded_around = jnp.pad(beside_all, ((0, 0), (0, 0), (0, 0), (1, 1), (0, 0)))
    diagonal = jnp.arange(slot_count)[:, None] == jnp.arange(slot_count)[None, :]

    def near_box(target_index):
        box_x = target_index // (2 * layers)
        box_y = target_index // layers % 2
        box_z = target_index % layers
        own_block = lax.dynamic_slice(
            packed, (0, box_x, box_y, box_z, 0), (4, 1, 1, 1, slot_count)
        ).reshape(4, slot_count)

        def stencil_term(stencil, running):
            move_x = stencil // 9 - 1
            move_y = stencil // 3 % 3 - 1
            move_z = stencil % 3 - 1
            source = lax.dynamic_slice(
                padded_around,
                (0, box_x + 1 + move_x, box_y + 1 + move_y, box_z + 1 + move_z, 0),
                (4, 1, 1, 1, slot_count),
            ).reshape(4, slot_count)
            delta_x = own_block[0][:, None] - source[0][None, :] - move_x.astype(jnp.float32)
            delta_y = own_block[1][:, None] - source[1][None, :] - move_y.astype(jnp.float32)
            delta_z = own_block[2][:, None] - source[2][None, :] - move_z.astype(jnp.float32)
            kernel = lax.rsqrt(
                delta_x * delta_x + delta_y * delta_y + delta_z * delta_z + softening_sq
            )
            kernel = jnp.where(diagonal & (stencil == 13), 0.0, kernel)
            return running + jnp.sum(kernel * source[3][None, :], axis=1)

        return lax.fori_loop(0, 27, stencil_term, jnp.zeros((slot_count,), jnp.float32))

    near = lax.map(near_box, jnp.arange(4 * layers)).reshape(2, 2, layers, slot_count)
    leaf_down_pts = 0.5 + 1.8 * unit_sphere
    leaf_far = point_sum(offsets, leaf_down_pts[:, None, None, None, :], leaf_local)
    parent_down_pts = 1.0 + 3.6 * unit_sphere
    local_float = local_index.astype(jnp.float32)
    layer_parity = (layer_index % 2).astype(jnp.float32)
    in_parent = jnp.stack(
        [
            local_float[:, None, None, None] + offsets[0],
            local_float[None, :, None, None] + offsets[1],
            layer_parity[None, None, :, None] + offsets[2],
        ]
    )
    spread_local = jnp.repeat(parent_local, 2, axis=0)[None, None]
    parent_far = point_sum(in_parent, parent_down_pts[:, None, None, None, :], spread_local)
    total = near + leaf_far + parent_far
    return jnp.where(slot_index < counts[..., None], total, 0.0)


def solution(mesh):
    return jax.shard_map(
        shards,
        mesh=mesh,
        in_specs=(
            P(None, "gx", "gy", None, None),
            P("gx", "gy", None, None),
            P("gx", "gy", None),
            P(),
            P(),
            P(),
            P(),
        ),
        out_specs=P("gx", "gy", None, None),
        check_vma=False,
    )
```

profile of v0, /device:TPU:1, one launch (start us, length us, event | category | flops | bytes accessed | tf_op | source)
XLA Modules:
  0.0 1413.7 jit_solution(3551635941989699017)
XLA Ops:
  17.0 610.7 %all-gather.2 = f32[256,2,256]{2,1,0:T(2,128)S(1)} all-gather(f32[1,2,256]{2,1,0:T(2,128)S(1)} %convolution_bitcast_fusion), channel_id=2, replica_groups=mesh['gx'=16,'gy'=16] {'gx','gy'}, dimensions={0}, use_global_device_ids=true | all-gather | bytes 526336 | tf_op jit(solution)/shard_map/all_gather | solution.py:147
  634.5 228.4 %while.64 = (s32[]{:T(128)}, f32[16,128]{1,0:T(8,128)S(1)}, s32[16]{0:T(128)S(1)}, f32[4,2,2,4,128]{4,0,3,2,1:T(4,128)S(1)}, f32[4,4,4,6,128]{4,3,2,1,0:T(8,128)...) while((s32[]{:T(128)}, f32[16,128]{1,0:T(8,128)S(1)}, ...), condition=%wide.region_4.5_spmd.clone, body=%wide.region_0.4_spmd.clone.sunk | while | flops 278759 | bytes 52315 | solution.py:200
  638.0 10.7 while.66
  652.3 10.7 while.66
  666.5 10.7 while.66
  680.8 10.7 while.66
  695.1 10.7 while.66
  709.4 10.7 while.66
  723.6 10.7 while.66
  737.9 10.7 while.66
  752.2 10.7 while.66
  766.5 10.7 while.66
  780.7 10.7 while.66
  795.0 10.7 while.66
  809.3 10.7 while.66
  823.6 10.7 while.66
  837.8 10.7 while.66
  852.1 10.7 while.66
  862.9 539.8 %while.65 = (s32[]{:T(128)}, f32[2,256]{1,0:T(2,128)S(1)}, f32[2,2,4,256]{3,2,1,0:T(4,128)S(1)}, s32[]{:T(128)}, s32[]{:T(128)}, /*index=5*/f32[256,2,256]{2,1,0...) while((s32[]{:T(128)}, f32[2,256]{1,0:T(2,128)S(1)}, ...), condition=%wide.region_11.12_spmd.clone.clone, body=%wide.region_7.11_spmd.clone.clone.sunk | while | flops 421864384 | bytes 7074936 | solution.py:166
  863.4 28.7 %conditional.4 = (f32[2,2,4,256]{3,2,1,0:T(4,128)S(1)}) conditional(s32[]{:T(128)} %convert_element_type.394, f32[2,2,4,256]{3,2,1,0:T(4,128)S(1)} %get-tuple-element.1713, (s32[]{:T(128)}, s32[2]{0:T(128)S(1)}, s32[]{:T(128)}, s32[2]{0:T(128)S(1)}, s32[7]{0:T(128)S(1)}, /*index=5*/s32[7]{0:T(128)S(1)}, s32[7]{0:T(128)S(1)}, s32[7]{0:T(128)S(1)}, ...), branch_computations={%region_9.9_spmd, %region_10.10_spmd.clone} | conditional | flops 419562336 | bytes 5998500 | solution.py:158
  865.6 6.5 fusion.85
  872.3 6.6 fusion.106
  879.0 6.6 fusion.103
  885.6 6.6 fusion.100
  893.3 28.7 %conditional.4 = (f32[2,2,4,256]{3,2,1,0:T(4,128)S(1)}) conditional(s32[]{:T(128)} %convert_element_type.394, f32[2,2,4,256]{3,2,1,0:T(4,128)S(1)} %get-tuple-element.1713, (s32[]{:T(128)}, s32[2]{0:T(128)S(1)}, s32[]{:T(128)}, s32[2]{0:T(128)S(1)}, s32[7]{0:T(128)S(1)}, /*index=5*/s32[7]{0:T(128)S(1)}, s32[7]{0:T(128)S(1)}, s32[7]{0:T(128)S(1)}, ...), branch_computations={%region_9.9_spmd, %region_10.10_spmd.clone} | conditional | flops 419562336 | bytes 5998500 | solution.py:158
  895.4 6.5 fusion.85
  902.1 6.6 fusion.106
  908.8 6.6 fusion.103
  915.4 6.6 fusion.100
  937.4 28.7 %conditional.4 = (f32[2,2,4,256]{3,2,1,0:T(4,128)S(1)}) conditional(s32[]{:T(128)} %convert_element_type.394, f32[2,2,4,256]{3,2,1,0:T(4,128)S(1)} %get-tuple-element.1713, (s32[]{:T(128)}, s32[2]{0:T(128)S(1)}, s32[]{:T(128)}, s32[2]{0:T(128)S(1)}, s32[7]{0:T(128)S(1)}, /*index=5*/s32[7]{0:T(128)S(1)}, s32[7]{0:T(128)S(1)}, s32[7]{0:T(128)S(1)}, ...), branch_computations={%region_9.9_spmd, %region_10.10_spmd.clone} | conditional | flops 419562336 | bytes 5998500 | solution.py:158
  939.5 6.5 fusion.85
  946.2 6.6 fusion.106
  952.9 6.6 fusion.103
  959.5 6.6 fusion.100
  967.2 28.7 %conditional.4 = (f32[2,2,4,256]{3,2,1,0:T(4,128)S(1)}) conditional(s32[]{:T(128)} %convert_element_type.394, f32[2,2,4,256]{3,2,1,0:T(4,128)S(1)} %get-tuple-element.1713, (s32[]{:T(128)}, s32[2]{0:T(128)S(1)}, s32[]{:T(128)}, s32[2]{0:T(128)S(1)}, s32[7]{0:T(128)S(1)}, /*index=5*/s32[7]{0:T(128)S(1)}, s32[7]{0:T(128)S(1)}, s32[7]{0:T(128)S(1)}, ...), branch_computations={%region_9.9_spmd, %region_10.10_spmd.clone} | conditional | flops 419562336 | bytes 5998500 | solution.py:158
  969.3 6.5 fusion.85
  976.1 6.6 fusion.106
  982.8 6.6 fusion.103
  989.3 6.6 fusion.100
  997.0 28.7 %conditional.4 = (f32[2,2,4,256]{3,2,1,0:T(4,128)S(1)}) conditional(s32[]{:T(128)} %convert_element_type.394, f32[2,2,4,256]{3,2,1,0:T(4,128)S(1)} %get-tuple-element.1713, (s32[]{:T(128)}, s32[2]{0:T(128)S(1)}, s32[]{:T(128)}, s32[2]{0:T(128)S(1)}, s32[7]{0:T(128)S(1)}, /*index=5*/s32[7]{0:T(128)S(1)}, s32[7]{0:T(128)S(1)}, s32[7]{0:T(128)S(1)}, ...), branch_computations={%region_9.9_spmd, %region_10.10_spmd.clone} | conditional | flops 419562336 | bytes 5998500 | solution.py:158
  999.2 6.5 fusion.85
  1005.9 6.6 fusion.106
  1012.6 6.6 fusion.103
  1019.2 6.6 fusion.100
  1041.1 28.7 %conditional.4 = (f32[2,2,4,256]{3,2,1,0:T(4,128)S(1)}) conditional(s32[]{:T(128)} %convert_element_type.394, f32[2,2,4,256]{3,2,1,0:T(4,128)S(1)} %get-tuple-element.1713, (s32[]{:T(128)}, s32[2]{0:T(128)S(1)}, s32[]{:T(128)}, s32[2]{0:T(128)S(1)}, s32[7]{0:T(128)S(1)}, /*index=5*/s32[7]{0:T(128)S(1)}, s32[7]{0:T(128)S(1)}, s32[7]{0:T(128)S(1)}, ...), branch_computations={%region_9.9_spmd, %region_10.10_spmd.clone} | conditional | flops 419562336 | bytes 5998500 | solution.py:158
  1043.3 6.5 fusion.85
  1050.0 6.6 fusion.106
  1056.7 6.6 fusion.103
  1063.3 6.6 fusion.100
  1070.9 28.7 %conditional.4 = (f32[2,2,4,256]{3,2,1,0:T(4,128)S(1)}) conditional(s32[]{:T(128)} %convert_element_type.394, f32[2,2,4,256]{3,2,1,0:T(4,128)S(1)} %get-tuple-element.1713, (s32[]{:T(128)}, s32[2]{0:T(128)S(1)}, s32[]{:T(128)}, s32[2]{0:T(128)S(1)}, s32[7]{0:T(128)S(1)}, /*index=5*/s32[7]{0:T(128)S(1)}, s32[7]{0:T(128)S(1)}, s32[7]{0:T(128)S(1)}, ...), branch_computations={%region_9.9_spmd, %region_10.10_spmd.clone} | conditional | flops 419562336 | bytes 5998500 | solution.py:158
  1073.1 6.5 fusion.85
  1079.8 6.6 fusion.106
  1086.5 6.6 fusion.103
  1093.1 6.6 fusion.100
  1100.8 28.7 %conditional.4 = (f32[2,2,4,256]{3,2,1,0:T(4,128)S(1)}) conditional(s32[]{:T(128)} %convert_element_type.394, f32[2,2,4,256]{3,2,1,0:T(4,128)S(1)} %get-tuple-element.1713, (s32[]{:T(128)}, s32[2]{0:T(128)S(1)}, s32[]{:T(128)}, s32[2]{0:T(128)S(1)}, s32[7]{0:T(128)S(1)}, /*index=5*/s32[7]{0:T(128)S(1)}, s32[7]{0:T(128)S(1)}, s32[7]{0:T(128)S(1)}, ...), branch_computations={%region_9.9_spmd, %region_10.10_spmd.clone} | conditional | flops 419562336 | bytes 5998500 | solution.py:158
  1102.9 6.5 fusion.85
  1109.6 6.6 fusion.106
  1116.4 6.6 fusion.103
  1122.9 6.6 fusion.100
  1144.9 28.7 %conditional.4 = (f32[2,2,4,256]{3,2,1,0:T(4,128)S(1)}) conditional(s32[]{:T(128)} %convert_element_type.394, f32[2,2,4,256]{3,2,1,0:T(4,128)S(1)} %get-tuple-element.1713, (s32[]{:T(128)}, s32[2]{0:T(128)S(1)}, s32[]{:T(128)}, s32[2]{0:T(128)S(1)}, s32[7]{0:T(128)S(1)}, /*index=5*/s32[7]{0:T(128)S(1)}, s32[7]{0:T(128)S(1)}, s32[7]{0:T(128)S(1)}, ...), branch_computations={%region_9.9_spmd, %region_10.10_spmd.clone} | conditional | flops 419562336 | bytes 5998500 | solution.py:158
  1147.0 6.5 fusion.85
  1153.7 6.6 fusion.106
  1160.5 6.6 fusion.103
  1167.0 6.6 fusion.100
  (5654 shorter events, 399.8 us)
Async XLA Ops:
  6.5 2.8 copy-start
  6.5 621.2 %copy-start.4 = (f32[3,2,2,4,128]{4,3,2,1,0:T(4,128)S(1)}, f32[3,2,2,4,128]{4,3,2,1,0:T(4,128)}, u32[]{:S(2)}) copy-start(f32[3,2,2,4,128]{4,3,2,1,0:T(4,128)} %param.15) | copy-start | bytes 73732
  6.5 10.2 copy-start.2
  6.5 856.4 %all-gather.5.cloned.1.call-start = ((), (), s32[]{:S(2)}) async-start(), calls=%async_computation | async-start | bytes 4210688 | tf_op jit(solution)/shard_map/all_gather | solution.py:146
  11.1 616.7 %collective-permute-start = (f32[4,1,2,4,128]{4,3,2,1,0:T(4,128)S(1)}, f32[4,1,2,4,128]{4,3,2,1,0:T(4,128)S(1)}, u32[]{:S(2)}, u32[]{:S(2)}) collective-permute-start(f32[4,1,2,4,128]{4,3,2,1,0:T(4,128)S(1)} %copy.42), channel_id=1, source_target_pairs={{0,16},{16,32},{32,48},{48,64},{64,80},{80,96},{96,112},{112,128},... | collective-permute-start | bytes 49160 | tf_op jit(solution)/shard_map/ppermute | solution.py:18
  13.9 614.0 %collective-permute-start.1 = (f32[4,1,2,4,128]{4,3,2,1,0:T(4,128)S(1)}, f32[4,1,2,4,128]{4,3,2,1,0:T(4,128)S(1)}, u32[]{:S(2)}, u32[]{:S(2)}) collective-permute-start(f32[4,1,2,4,128]{4,3,2,1,0:T(4,128)S(1)} %copy.43), channel_id=1, source_target_pairs={{16,0},{32,16},{48,32},{64,48},{80,64},{96,80},{112,96},{128,112},... | collective-permute-start | bytes 49160 | tf_op jit(solution)/shard_map/ppermute | solution.py:20
  627.9 6.5 collective-permute-start.2
  628.0 6.4 collective-permute-start.3
  862.9 539.9 %copy-start.1 = (f32[256,256]{1,0:T(8,128)S(1)}, f32[256,256]{1,0:T(8,128)}, u32[]{:S(2)}) copy-start(f32[256,256]{1,0:T(8,128)} %param.19) | copy-start | bytes 786436
  862.9 541.5 %copy-start.3 = (f32[256,256]{1,0:T(8,128)S(1)}, f32[256,256]{1,0:T(8,128)}, u32[]{:S(2)}) copy-start(f32[256,256]{1,0:T(8,128)} %param.21) | copy-start | bytes 786436
  862.9 543.2 %copy-start.5 = (s32[2,2,4]{2,1,0:T(2,128)S(1)}, s32[2,2,4]{2,1,0:T(2,128)}, u32[]{:S(2)}) copy-start(s32[2,2,4]{2,1,0:T(2,128)} %param.17) | copy-start | bytes 196
Sparse Core Ops, SparseCore 0:
  10.4 721.4 all-gather.4
where the time goes:
time: 1430 us; the launch traced here: 1410 us
  blocking collectives  611 us (43%)
  other arithmetic  342 us (24%)
  matrix products  238 us (17%)
  loops' own time  156 us (11%)
  local copies, waits for them, and re-layouts  42.4 us (3%)
    all_gather x1, blocking collectives, shards(): lax.all_gather(parent_eq[None], ('gx', 'gy'), axis=0, tiled=True)  611 us
    dot_general x36, matrix products, neighbour_leaves(): jnp.einsum('ijzce,ijzke->ijkc', matrices, sources, precision=highest)  236 us
    reduce_sum x256, other arithmetic, far_term(): return keep * jnp.sum(matrices * density[None, :, None, :], axis=(1, 3))  99.3 us
    reduce_sum x432, other arithmetic, stencil_term(): return running + jnp.sum(kernel * source[3][None, :], axis=1)  90.1 us
    another operation x16, loops' own time, near_box(): lax.fori_loop(0, 27, stencil_term, jnp.zeros((slot_count,), jnp.float32))  64.7 us
    another operation x1, loops' own time, shards(): lax.map(near_box, jnp.arange(4 * layers)).reshape(2, 2, layers, slot_count)  45.4 us
    another operation x1, loops' own time, shards(): lax.fori_loop(0, parent_piece.shape[0], one_source, start_carry)  41.7 us
    add x256, other arithmetic, translation(): delta_x * delta_x + delta_y * delta_y + delta_z * delta_z + softening_sq  37.6 us

commit v1 on v0

v1 whole, which is shorter than its diff:
```python
import functools

import jax
import jax.numpy as jnp
import numpy as np
from jax import lax
from jax.experimental import pallas as pl
from jax.experimental.pallas import tpu as pltpu
from jax.sharding import PartitionSpec as P

SOFT = 0.0004
F32 = jnp.float32
BF16 = jnp.bfloat16
HIGHEST = lax.Precision.HIGHEST
MESH = pl.DeviceIdType.MESH


def sphere_points(count):
    middle = np.arange(count).astype(np.float32) + np.float32(0.5)
    height = (np.float32(1.0) - np.float32(2.0) * middle / np.float32(count)).astype(np.float32)
    radial = np.sqrt(np.maximum(np.float32(1.0) - height * height, np.float32(0.0)))
    turn = (middle * np.float32(2.399963229728653)).astype(np.float32)
    cos = np.cos(turn.astype(np.float64)).astype(np.float32)
    sin = np.sin(turn.astype(np.float64)).astype(np.float32)
    return np.stack([radial * cos, radial * sin, height]).astype(np.float32)


def split(value):
    high = value.astype(BF16)
    low = (value - high.astype(F32)).astype(BF16)
    return high, low


def bdot(a, b):
    return jnp.dot(a, b, preferred_element_type=F32)


def dot_t(a, b):
    return lax.dot_general(
        a, b, (((1,), (1,)), ((), ())), precision=HIGHEST, preferred_element_type=F32
    )


def leaf_task(a):
    return a // 2 - 3, a % 2


def body(
    nx,
    ny,
    counts_ref,
    off_ref,
    chg_ref,
    u_ref,
    ut_ref,
    cl_up,
    cl_down,
    ct_up,
    ct_down,
    out_ref,
    halo,
    tables,
    k_leaf,
    k_parent,
    up_hi,
    up_lo,
    leaf_send,
    leaf_recv,
    par_send,
    par_recv,
    rs_send,
    rs_recv,
    shifted,
    par_ring,
    m_hi,
    m_lo,
    l_hi,
    l_lo,
    near_acc,
    turned_ref,
    halo_ssem,
    halo_rsem,
    leaf_ssem,
    leaf_rsem,
    par_ssem,
    par_rsem,
    rs_ssem,
    rs_rsem,
):
    a = lax.axis_index("gx")
    b = lax.axis_index("gy")
    lane128 = lax.broadcasted_iota(jnp.int32, (4, 128), 1)

    for px in range(2):
        for py in range(2):
            cell = halo.at[1 + px, 1 + py]
            for comp in range(3):
                cell[4 * comp : 4 * comp + 4, :] = off_ref[comp, px, py]
            for k in range(4):
                row = chg_ref[px, py, k : k + 1, :]
                cell[12 + k : 13 + k, :] = jnp.where(
                    lane128[0:1] < counts_ref[px, py, k], row, 0.0
                )

    sides = [(sx, sy) for sx in (-1, 0, 1) for sy in (-1, 0, 1) if (sx, sy) != (0, 0)]

    def halo_copy(index):
        sx, sy = sides[index]
        src_x = pl.ds(1, 2) if sx == 0 else pl.ds(2 if sx == 1 else 1, 1)
        src_y = pl.ds(1, 2) if sy == 0 else pl.ds(2 if sy == 1 else 1, 1)
        dst_x = pl.ds(1, 2) if sx == 0 else pl.ds(0 if sx == 1 else 3, 1)
        dst_y = pl.ds(1, 2) if sy == 0 else pl.ds(0 if sy == 1 else 3, 1)
        return pltpu.make_async_remote_copy(
            src_ref=halo.at[src_x, src_y],
            dst_ref=halo.at[dst_x, dst_y],
            send_sem=halo_ssem.at[index],
            recv_sem=halo_rsem.at[index],
            device_id=(lax.rem(a + sx + nx, nx), lax.rem(b + sy + ny, ny)),
            device_id_type=MESH,
        )

    for index in range(8):
        halo_copy(index).start()

    for chunk in range(8):
        rows = pl.ds(32 * chunk, 32)
        total = jnp.zeros((32, 256), F32)
        for comp in range(3):
            diff = 0.9 * (u_ref[comp : comp + 1, :] - ut_ref[rows, comp : comp + 1])
            tables[1 + comp, rows, :] = -2.0 * diff
            total = total + diff * diff
        tables[0, rows, :] = total

    def child_chunk(chunk, carry):
        rows = pl.ds(pl.multiple_of(32 * chunk, 32), 32)
        base = jnp.full((32, 256), 0.1875 + SOFT / 4, F32)
        half = []
        for comp in range(3):
            diff = 1.8 * u_ref[comp : comp + 1, :] - 0.45 * ut_ref[rows, comp : comp + 1]
            base = base + diff * diff
            half.append(0.5 * diff)
        for child in range(8):
            value = base
            for comp, bit in enumerate((child // 4, child // 2 % 2, child % 2)):
                value = value + half[comp] if bit == 0 else value - half[comp]
            high, low = split(lax.rsqrt(value))
            up_hi[child, rows, :] = high
            up_lo[child, rows, :] = low
        return carry

    lax.fori_loop(0, 8, child_chunk, 0)

    centre = [0.5 + 1.8 * u_ref[comp : comp + 1, :] for comp in range(3)]
    checks = []
    for px in range(2):
        for py in range(2):
            turned = jnp.transpose(halo[1 + px, 1 + py])
            for k in range(4):
                box = (px * 2 + py) * 4 + k
                total = jnp.full((128, 256), SOFT, F32)
                for comp in range(3):
                    diff = centre[comp] - turned[:, 4 * comp + k : 4 * comp + k + 1]
                    total = total + diff * diff
                kernel = lax.rsqrt(total)
                k_leaf[box] = kernel
                weight = turned[:, 12 + k : 13 + k]
                checks.append(jnp.sum(kernel * weight, axis=0, keepdims=True))
    leaf_check = jnp.concatenate(checks, axis=0)
    leaf_eq = dot_t(leaf_check, cl_up[...])
    for px in range(2):
        for py in range(2):
            first = (px * 2 + py) * 4
            leaf_send[py, 4 * px : 4 * px + 4, :] = leaf_eq[first : first + 4, :]

    def leaf_route(target, py):
        dy, _ = leaf_task(target)
        src = py + dy
        valid = (target < 14) & (src >= -2) & (src <= 3)
        row = (src + 4) // 2 - 2
        return valid, row, (src + 4) % 2

    def leaf_copy(target, py):
        valid, row, src_py = leaf_route(target, py)
        to_b = lax.rem(b - row + ny, ny)
        copy = pltpu.make_async_remote_copy(
            src_ref=leaf_send.at[src_py],
            dst_ref=leaf_recv.at[a, py],
            send_sem=leaf_ssem.at[target, py],
            recv_sem=leaf_rsem.at[a, py],
            device_id=(target, to_b),
            device_id_type=MESH,
        )
        self_copy = (target == a) & (to_b == b)
        return valid, self_copy, src_py, copy

    def leaf_start(target, carry):
        for py in range(2):
            valid, self_copy, src_py, copy = leaf_copy(target, py)

            @pl.when(valid & jnp.logical_not(self_copy))
            def _():
                copy.start()

            @pl.when(valid & self_copy)
            def _():
                leaf_recv[a, py] = leaf_send[src_py]

        return carry

    lax.fori_loop(0, nx, leaf_start, 0)

    eq_hi, eq_lo = split(leaf_eq)
    both = jnp.concatenate([eq_hi, eq_lo], axis=0)
    row16 = lax.broadcasted_iota(jnp.int32, (16, 256), 0)
    rows_sum = jnp.zeros((16, 256), F32)
    for child in range(8):
        first = bdot(both, up_hi[child])
        term = first[:16] + first[16:] + bdot(eq_hi, up_lo[child])
        mine = ((row16 // 4) == (child // 2)) & ((row16 % 2) == (child % 2))
        rows_sum = jnp.where(mine, term, rows_sum)
    upper = (row16 % 4) >= 2
    check0 = 0.5 * jnp.sum(jnp.where(upper, 0.0, rows_sum), axis=0, keepdims=True)
    check1 = 0.5 * jnp.sum(jnp.where(upper, rows_sum, 0.0), axis=0, keepdims=True)
    row8 = lax.broadcasted_iota(jnp.int32, (8, 256), 0)
    parent_check = jnp.where(row8 == 0, check0, jnp.where(row8 == 1, check1, 0.0))
    par_send[...] = dot_t(parent_check, ct_up[...])

    def par_copy(target):
        to_b = lax.rem(b - target + nx // 2 + ny, ny)
        copy = pltpu.make_async_remote_copy(
            src_ref=par_send,
            dst_ref=par_recv.at[a],
            send_sem=par_ssem.at[target],
            recv_sem=par_rsem.at[a],
            device_id=(target, to_b),
            device_id_type=MESH,
        )
        return (target == a) & (to_b == b), copy

    def par_start(target, carry):
        self_copy, copy = par_copy(target)

        @pl.when(jnp.logical_not(self_copy))
        def _():
            copy.start()

        @pl.when(self_copy)
        def _():
            par_recv[a] = par_send[...]

        return carry

    lax.fori_loop(0, nx, par_start, 0)

    sub8 = lax.broadcasted_iota(jnp.int32, (8, 128), 0)
    lane8 = lax.broadcasted_iota(jnp.int32, (8, 128), 1)

    def near_column(fx, fy):
        turned_ref[...] = jnp.transpose(halo[fx, fy])
        columns = [
            (px, py)
            for px in range(2)
            for py in range(2)
            if abs(px + 1 - fx) <= 1 and abs(py + 1 - fy) <= 1
        ]
        pairs = [(px, py, k) for px, py in columns for k in range(4)]

        def tile(t, carry):
            sums = list(carry)
            block = turned_ref[pl.ds(pl.multiple_of(8 * t, 8), 8), :]
            for ks in range(4):
                source = [
                    jnp.broadcast_to(block[:, 4 * comp + ks : 4 * comp + ks + 1], (8, 128))
                    for comp in range(4)
                ]
                for slot, (px, py, k) in enumerate(pairs):
                    if abs(k - ks) > 1:
                        continue
                    shift = (px + 1 - fx, py + 1 - fy, k - ks)
                    total = None
                    for comp in range(3):
                        row = halo[1 + px, 1 + py, 4 * comp + k : 4 * comp + k + 1, :]
                        if shift[comp]:
                            row = row + float(shift[comp])
                        diff = row - source[comp]
                        total = diff * diff + SOFT if total is None else total + diff * diff
                    kernel = lax.rsqrt(total)
                    if shift == (0, 0, 0):
                        kernel = jnp.where(lane8 == sub8 + 8 * t, 0.0, kernel)
                    sums[slot] = sums[slot] + kernel * source[3]
            return tuple(sums)

        start = tuple(near_acc[(px * 2 + py) * 4 + k] for px, py, k in pairs)
        done = lax.fori_loop(0, 16, tile, start)
        for slot, (px, py, k) in enumerate(pairs):
            near_acc[(px * 2 + py) * 4 + k] = done[slot]

    near_acc[...] = jnp.zeros_like(near_acc)
    for fx in (1, 2):
        for fy in (1, 2):
            near_column(fx, fy)

    for px in range(2):
        for py in range(2):
            turned = jnp.transpose(halo[1 + px, 1 + py])
            for k in range(4):
                box = (px * 2 + py) * 4 + k
                total = jnp.full((128, 256), SOFT / 4, F32)
                for comp, bit in enumerate((px, py, k % 2)):
                    place = 0.5 * turned[:, 4 * comp + k : 4 * comp + k + 1] + 0.5 * bit
                    diff = centre[comp] - place
                    total = total + diff * diff
                k_parent[box] = lax.rsqrt(total)

    def par_wait(source, carry):
        from_b = lax.rem(b + a - nx // 2 + ny, ny)
        self_copy = (source == a) & (from_b == b)
        arrived = pltpu.make_async_remote_copy(
            src_ref=par_send,
            dst_ref=par_recv.at[source],
            send_sem=par_ssem.at[source],
            recv_sem=par_rsem.at[source],
            device_id=(lax.rem(a + 1, nx), b),
            device_id_type=MESH,
        )

        @pl.when(jnp.logical_not(self_copy))
        def _():
            arrived.wait_recv()

        return carry

    lax.fori_loop(0, nx, par_wait, 0)
    for source in range(nx):
        for layer in range(2):
            par_ring[layer, source : source + 1, :] = par_recv[source, layer : layer + 1, :]

    oy = a - nx // 2
    oy_f = oy.astype(F32)

    def far_step(index, carry):
        acc0, acc1 = carry
        ox = index - nx // 2
        ox_f = ox.astype(F32)
        keep = (ox > 1) | (ox < -1) | (oy > 1) | (oy < -1)
        const = ox_f * ox_f + oy_f * oy_f + SOFT / 4
        for chunk in range(8):
            rows = pl.ds(32 * chunk, 32)
            flat = tables[0, rows, :] + ox_f * tables[1, rows, :] + oy_f * tables[2, rows, :]
            flat = flat + const
            lift = tables[3, rows, :]
            for slot, value in enumerate((flat + 1.0 - lift, flat, flat + 1.0 + lift)):
                high, low = split(jnp.where(keep, lax.rsqrt(value), 0.0))
                m_hi[slot, rows, :] = high
                m_lo[slot, rows, :] = low
        turn = lax.rem(nx + nx // 2 - index, nx)
        p0h, p0l = split(pltpu.roll(par_ring[0], turn, 0))
        p1h, p1l = split(pltpu.roll(par_ring[1], turn, 0))
        same = bdot(jnp.concatenate([p0h, p1h, p0l, p1l], axis=0), m_hi[1])
        same2 = bdot(jnp.concatenate([p0h, p1h], axis=0), m_lo[1])
        up = bdot(jnp.concatenate([p1h, p1l], axis=0), m_hi[2])
        up2 = bdot(p1h, m_lo[2])
        down = bdot(jnp.concatenate([p0h, p0l], axis=0), m_hi[0])
        down2 = bdot(p0h, m_lo[0])
        acc0 = acc0 + ((same[0:16] + up[0:16]) + (same[32:48] + same2[0:16] + up[16:32] + up2))
        acc1 = acc1 + (
            (same[16:32] + down[0:16]) + (same[48:64] + same2[16:32] + down[16:32] + down2)
        )
        return acc0, acc1

    zero16 = jnp.zeros((16, 256), F32)
    far0, far1 = lax.fori_loop(0, nx, far_step, (zero16, zero16))
    for target in range(nx):
        rs_send[target, 2] = jnp.where(
            row8 == 0,
            0.5 * far0[target : target + 1, :],
            jnp.where(row8 == 1, 0.5 * far1[target : target + 1, :], 0.0),
        )

    dy, half_z = leaf_task(a)

    def leaf_wait(source, carry):
        for py in range(2):
            valid, row, src_py = leaf_route(a, py)
            self_copy = (source == a) & (row == 0)
            arrived = pltpu.make_async_remote_copy(
                src_ref=leaf_send.at[0],
                dst_ref=leaf_recv.at[source, py],
                send_sem=leaf_ssem.at[source, py],
                recv_sem=leaf_rsem.at[source, py],
                device_id=(lax.rem(a + 1, nx), b),
                device_id_type=MESH,
            )

            @pl.when(valid & jnp.logical_not(self_copy))
            def _():
                arrived.wait_recv()

        return carry

    lax.fori_loop(0, nx, leaf_wait, 0)

    @pl.when(dy == 3)
    def _():
        leaf_recv[:, 1] = jnp.zeros((nx, 8, 256), F32)

    @pl.when(dy == -3)
    def _():
        leaf_recv[:, 0] = jnp.zeros((nx, 8, 256), F32)

    for target in range(nx):
        rs_send[target, 0] = jnp.zeros((8, 256), F32)
        rs_send[target, 1] = jnp.zeros((8, 256), F32)

    @pl.when(a < 14)
    def _():
        for source in range(nx):
            low_py = leaf_recv[source, 0]
            high_py = leaf_recv[source, 1]
            first = row8 < 4
            shifted[0, 8 * source : 8 * source + 8, :] = jnp.where(
                first, low_py, pltpu.roll(high_py, 4, 0)
            )
            shifted[1, 8 * source : 8 * source + 8, :] = jnp.where(
                first, pltpu.roll(low_py, 4, 0), high_py
            )
        dy_f = dy.astype(F32)
        row128 = lax.broadcasted_iota(jnp.int32, (128, 256), 0) % 4

        def leaf_step(step, carry):
            dz = jnp.where(half_z == 0, step - 3, step + 1)

            @pl.when(dz <= 3)
            def _():
                dz_f = dz.astype(F32)
                beside = (dy >= -1) & (dy <= 1) & (dz >= -1) & (dz <= 1)
                const = dy_f * dy_f + dz_f * dz_f + SOFT
                for chunk in range(8):
                    rows = pl.ds(32 * chunk, 32)
                    base = tables[0, rows, :] + dy_f * tables[2, rows, :]
                    base = base + dz_f * tables[3, rows, :] + const
                    along = tables[1, rows, :]
                    for slot in range(7):
                        dx = slot - 3
                        value = base + (float(dx) * along + float(dx * dx)) if dx else base
                        kernel = lax.rsqrt(value)
                        if abs(dx) <= 1:
                            kernel = jnp.where(beside, 0.0, kernel)
                        high, low = split(kernel)
                        m_hi[slot, rows, :] = high
                        m_lo[slot, rows, :] = low
                inside = (row128 + dz >= 0) & (row128 + dz <= 3)
                turn = lax.rem(128 - dz, 128)
                for sx in range(2):
                    moved = jnp.where(inside, pltpu.roll(shifted[sx], turn, 0), 0.0)
                    for block in (-1, 0, 1):
                        if block == -1:
                            placed = jnp.concatenate([moved[120:], moved[:120]], axis=0)
                        elif block == 1:
                            placed = jnp.concatenate([moved[8:], moved[:8]], axis=0)
                        else:
                            placed = moved
                        slot = 2 * block + sx + 2
                        high, low = split(placed)
                        l_hi[slot] = high
                        l_lo[slot] = low
                for px in range(2):
                    total = jnp.zeros((128, 256), F32)
                    for slot in range(6):
                        matrix = slot + 1 - px
                        total = total + (
                            bdot(l_hi[slot], m_hi[matrix])
                            + (bdot(l_lo[slot], m_hi[matrix]) + bdot(l_hi[slot], m_lo[matrix]))
                        )
                    rs_send[:, px] = rs_send[:, px] + total.reshape(nx, 8, 256)

            return carry

        lax.fori_loop(0, 4, leaf_step, 0)

    def rs_copy(target):
        return pltpu.make_async_remote_copy(
            src_ref=rs_send.at[target],
            dst_ref=rs_recv.at[a],
            send_sem=rs_ssem.at[target],
            recv_sem=rs_rsem.at[a],
            device_id=(target, b),
            device_id_type=MESH,
        )

    def rs_start(step, carry):
        rs_copy(lax.rem(a + step, nx)).start()
        return carry

    lax.fori_loop(1, nx, rs_start, 0)
    rs_recv[a] = rs_send[a]

    for index in range(8):
        halo_copy(7 - index).wait_recv()
    for fx in range(4):
        for fy in range(4):
            if fx in (0, 3) or fy in (0, 3):
                near_column(fx, fy)

    def rs_wait(step, carry):
        source = lax.rem(a + step, nx)
        pltpu.make_async_remote_copy(
            src_ref=rs_send.at[source],
            dst_ref=rs_recv.at[source],
            send_sem=rs_ssem.at[source],
            recv_sem=rs_rsem.at[source],
            device_id=(source, b),
            device_id_type=MESH,
        ).wait_recv()
        return carry

    lax.fori_loop(1, nx, rs_wait, 0)
    sums = [jnp.zeros((8, 256), F32) for _ in range(3)]
    for source in range(nx):
        for part in range(3):
            sums[part] = sums[part] + rs_recv[source, part]

    leaf_local = dot_t(jnp.concatenate([sums[0], sums[1]], axis=0), cl_down[...])
    parent_local = 0.5 * dot_t(sums[2], ct_down[...])
    lanes = lax.broadcasted_iota(jnp.int32, (128, 128), 1)
    columns = jnp.zeros((128, 128), F32)
    for box in range(16):
        layer = (box % 4) // 2
        value = k_leaf[box] * leaf_local[box : box + 1, :]
        value = value + k_parent[box] * parent_local[layer : layer + 1, :]
        column = jnp.sum(value, axis=1, keepdims=True)
        columns = jnp.where(lanes == box, column, columns)
    flipped = jnp.transpose(columns)
    for px in range(2):
        for py in range(2):
            for k in range(4):
                box = (px * 2 + py) * 4 + k
                row = flipped[box : box + 1, :] + jnp.sum(near_acc[box], axis=0, keepdims=True)
                out_ref[px, py, k : k + 1, :] = jnp.where(
                    lane128[0:1] < counts_ref[px, py, k], row, 0.0
                )

    for index in range(8):
        halo_copy(index).wait_send()

    def drain(target, carry):
        for py in range(2):
            valid, self_copy, _, copy = leaf_copy(target, py)

            @pl.when(valid & jnp.logical_not(self_copy))
            def _():
                copy.wait_send()

        own, copy = par_copy(target)

        @pl.when(jnp.logical_not(own))
        def _():
            copy.wait_send()

        @pl.when(target != a)
        def _():
            rs_copy(target).wait_send()

        return carry

    lax.fori_loop(0, nx, drain, 0)


def shards(offsets, charges, counts, cl_up, cl_down, ct_up, ct_down):
    nx = lax.axis_size("gx")
    ny = lax.axis_size("gy")
    points = sphere_points(256)
    unit = np.zeros((8, 256), np.float32)
    unit[:3] = points
    unit_t = np.zeros((256, 8), np.float32)
    unit_t[:, :3] = points.T
    vmem = pl.BlockSpec(memory_space=pltpu.VMEM)
    dma = pltpu.SemaphoreType.DMA
    return pl.pallas_call(
        functools.partial(body, nx, ny),
        out_shape=jax.ShapeDtypeStruct(charges.shape, F32),
        in_specs=[pl.BlockSpec(memory_space=pltpu.SMEM)] + [vmem] * 8,
        out_specs=vmem,
        scratch_shapes=[
            pltpu.VMEM((4, 4, 16, 128), F32),
            pltpu.VMEM((4, 256, 256), F32),
            pltpu.VMEM((16, 128, 256), F32),
            pltpu.VMEM((16, 128, 256), F32),
            pltpu.VMEM((8, 256, 256), BF16),
            pltpu.VMEM((8, 256, 256), BF16),
            pltpu.VMEM((2, 8, 256), F32),
            pltpu.VMEM((nx, 2, 8, 256), F32),
            pltpu.VMEM((8, 256), F32),
            pltpu.VMEM((nx, 8, 256), F32),
            pltpu.VMEM((nx, 3, 8, 256), F32),
            pltpu.VMEM((nx, 3, 8, 256), F32),
            pltpu.VMEM((2, 8 * nx, 256), F32),
            pltpu.VMEM((2, nx, 256), F32),
            pltpu.VMEM((7, 256, 256), BF16),
            pltpu.VMEM((7, 256, 256), BF16),
            pltpu.VMEM((6, 8 * nx, 256), BF16),
            pltpu.VMEM((6, 8 * nx, 256), BF16),
            pltpu.VMEM((16, 8, 128), F32),
            pltpu.VMEM((128, 16), F32),
            dma((8,)),
            dma((8,)),
            dma((nx, 2)),
            dma((nx, 2)),
            dma((nx,)),
            dma((nx,)),
            dma((nx,)),
            dma((nx,)),
        ],
        compiler_params=pltpu.CompilerParams(
            has_side_effects=True, vmem_limit_bytes=48 * 1024 * 1024
        ),
        name="multipole",
    )(counts, offsets, charges, jnp.asarray(unit), jnp.asarray(unit_t), cl_up, cl_down, ct_up, ct_down)


def solution(mesh):
    return jax.shard_map(
        shards,
        mesh=mesh,
        in_specs=(
            P(None, "gx", "gy", None, None),
            P("gx", "gy", None, None),
            P("gx", "gy", None),
            P(),
            P(),
            P(),
            P(),
        ),
        out_specs=P("gx", "gy", None, None),
        check_vma=False,
    )
```

time: 1430 us -> 76.4 us (0.05); the launches traced: 1410 us -> 76 us
  blocking collectives: 611 us -> 0 us
  other arithmetic: 342 us -> 0 us
  matrix products: 238 us -> 0 us
  loops' own time: 156 us -> 0 us
  Pallas kernels: 0 us -> 67.8 us
  local copies, waits for them, and re-layouts: 42.4 us -> 8.11 us
    all_gather x1 -> x0, blocking collectives: 611 us -> none  [shards(): lax.all_gather(parent_eq[None], ('gx', 'gy'), axis=0, tiled=True)]
    dot_general x40 -> x0, matrix products: 238 us -> none  [the longest x36 236 us: neighbour_leaves(): jnp.einsum('ijzce,ijzke->ijkc', matrices, sources, precision=highest)]
    reduce_sum x692 -> x0, other arithmetic: 194 us -> none  [the longest x256 99.3 us: far_term(): return keep * jnp.sum(matrices * density[None, :, None, :], axis=(1, 3))]
    another operation x274 -> x0, loops' own time: 156 us -> none  [the longest x16 64.7 us: near_box(): lax.fori_loop(0, 27, stencil_term, jnp.zeros((slot_count,), jnp.float32))]
    mul x1064 -> x0, other arithmetic: 74.9 us -> none  [the longest x265 27.1 us: translation(): radius * (unit_sphere[2][:, None] - unit_sphere[2][None, :])]
    pallas_call x0 -> x1, Pallas kernels: none -> 67.8 us  [shards(): pl.pallas_call(functools.partial(body, nx, ny), out_shape=jax.ShapeDtypeS...]
    add x1204 -> x0, other arithmetic: 64.3 us -> none  [the longest x256 37.6 us: translation(): delta_x * delta_x + delta_y * delta_y + delta_z * delta_z + softening_sq]
where the time goes in v1:
time: 76.4 us; the launch traced here: 76 us
  Pallas kernels  67.8 us (89%)
  local copies, waits for them, and re-layouts  8.11 us (11%)
    pallas_call x1, Pallas kernels, shards(): pl.pallas_call(functools.partial(body, nx, ny), out_shape=jax.ShapeDtypeS...  67.8 us
    unnamed x19, local copies, waits for them, and re-layouts  8.11 us

profile of v1, /device:TPU:1, one launch (start us, length us, event | category | flops | bytes accessed | tf_op | source)
XLA Modules:
  0.0 76.0 jit_solution(12579008444100914868)
XLA Ops:
  0.0 0.0 copy-start
  0.0 0.9 %copy-done = f32[256,256]{1,0:T(8,128)S(1)} copy-done((f32[256,256]{1,0:T(8,128)S(1)}, f32[256,256]{1,0:T(8,128)}, u32[]{:S(2)}) %copy-start) | copy-done | bytes 262168
  1.0 0.0 copy-start.1
  1.0 0.9 %copy-done.1 = f32[256,256]{1,0:T(8,128)S(1)} copy-done((f32[256,256]{1,0:T(8,128)S(1)}, f32[256,256]{1,0:T(8,128)}, u32[]{:S(2)}) %copy-start.1) | copy-done | bytes 262168
  1.9 0.0 copy-start.2
  1.9 0.9 %copy-done.2 = f32[256,256]{1,0:T(8,128)S(1)} copy-done((f32[256,256]{1,0:T(8,128)S(1)}, f32[256,256]{1,0:T(8,128)}, u32[]{:S(2)}) %copy-start.2) | copy-done | bytes 262168
  2.9 0.0 copy-start.3
  2.9 0.9 %copy-done.3 = f32[256,256]{1,0:T(8,128)S(1)} copy-done((f32[256,256]{1,0:T(8,128)S(1)}, f32[256,256]{1,0:T(8,128)}, u32[]{:S(2)}) %copy-start.3) | copy-done | bytes 262168
  3.8 0.0 copy-start.4
  3.8 0.9 %copy-done.4 = f32[256,8]{1,0:T(8,128)S(1)} copy-done((f32[256,8]{1,0:T(8,128)S(1)}, f32[256,8]{1,0:T(8,128)}, u32[]{:S(2)}) %copy-start.4) | copy-done | bytes 8216
  4.7 0.0 copy-start.5
  4.7 0.7 copy-done.5
  5.4 0.0 copy-start.6
  5.4 0.7 copy-done.6
  6.1 0.0 copy-start.7
  6.1 0.7 copy-done.7
  6.8 0.0 copy-start.8
  6.8 0.7 copy-done.8
  7.5 67.8 %multipole.1 = f32[2,2,4,128]{3,2,1,0:T(4,128)S(1)} custom-call(s32[2,2,4]{2,1,0:T(2,128)S(1)} %copy-done.8, f32[3,2,2,4,128]{4,3,2,1,0:T(4,128)S(1)} %copy-done.5, f32[2,2,4,128]{3,2,1,0:T(4,128)S(1)} %copy-done.6, f32[8,256]{1,0:T(8,128)S(1)} %copy-done.7, f32[256,8]{1,0:T(8,128)S(1)} %copy-done.4, f32[256,256]{1,0:T(8,128)S(1)} %copy-done, ...), custom_call_target="tpu_custom_call" | custom-call | tf_op jit(solution)/shard_map/multipole/pallas_call | solution.py:579
  75.4 0.6 copy.11
Async XLA Ops:
  0.0 0.9 %copy-start = (f32[256,256]{1,0:T(8,128)S(1)}, f32[256,256]{1,0:T(8,128)}, u32[]{:S(2)}) copy-start(f32[256,256]{1,0:T(8,128)} %cl_up.1) | copy-start | bytes 786436
  1.0 0.9 %copy-start.1 = (f32[256,256]{1,0:T(8,128)S(1)}, f32[256,256]{1,0:T(8,128)}, u32[]{:S(2)}) copy-start(f32[256,256]{1,0:T(8,128)} %cl_down.1) | copy-start | bytes 786436
  1.9 0.9 %copy-start.2 = (f32[256,256]{1,0:T(8,128)S(1)}, f32[256,256]{1,0:T(8,128)}, u32[]{:S(2)}) copy-start(f32[256,256]{1,0:T(8,128)} %ct_up.1) | copy-start | bytes 786436
  2.9 0.9 %copy-start.3 = (f32[256,256]{1,0:T(8,128)S(1)}, f32[256,256]{1,0:T(8,128)}, u32[]{:S(2)}) copy-start(f32[256,256]{1,0:T(8,128)} %ct_down.1) | copy-start | bytes 786436
  3.8 0.9 %copy-start.4 = (f32[256,8]{1,0:T(8,128)S(1)}, f32[256,8]{1,0:T(8,128)}, u32[]{:S(2)}) copy-start(f32[256,8]{1,0:T(8,128)} %constant.5.clone.ut_ref) | copy-start | bytes 24580
  4.7 0.7 copy-start.5
  5.4 0.7 copy-start.6
  6.1 0.7 copy-start.7
  6.8 0.7 copy-start.8

commit v2 on v1

--- a/solution.py
+++ b/solution.py
@@ -13,6 +13,7 @@
 BF16 = jnp.bfloat16
 HIGHEST = lax.Precision.HIGHEST
 MESH = pl.DeviceIdType.MESH
+SIDES = [(sx, sy) for sx in (-1, 0, 1) for sy in (-1, 0, 1) if (sx, sy) != (0, 0)]
 
 
 def sphere_points(count):
@@ -48,6 +49,16 @@
 def body(
     nx,
     ny,
+    counts_hbm,
+    off_hbm,
+    chg_hbm,
+    u_hbm,
+    ut_hbm,
+    cl_up_hbm,
+    cl_down_hbm,
+    ct_up_hbm,
+    ct_down_hbm,
+    out_ref,
     counts_ref,
     off_ref,
     chg_ref,
@@ -57,7 +68,7 @@
     cl_down,
     ct_up,
     ct_down,
-    out_ref,
+    in_sem,
     halo,
     tables,
     k_leaf,
@@ -91,6 +102,58 @@
     b = lax.axis_index("gy")
     lane128 = lax.broadcasted_iota(jnp.int32, (4, 128), 1)
 
+    fetches = [
+        pltpu.make_async_copy(src, dst, in_sem.at[index])
+        for index, (src, dst) in enumerate(
+            (
+                (counts_hbm, counts_ref),
+                (off_hbm, off_ref),
+                (chg_hbm, chg_ref),
+                (u_hbm, u_ref),
+                (ut_hbm, ut_ref),
+                (cl_up_hbm, cl_up),
+                (ct_up_hbm, ct_up),
+                (cl_down_hbm, cl_down),
+                (ct_down_hbm, ct_down),
+            )
+        )
+    ]
+    for fetch in fetches:
+        fetch.start()
+
+    barrier = pltpu.get_barrier_semaphore()
+
+    def hello(to_a, to_b):
+        pl.semaphore_signal(barrier, inc=1, device_id=(to_a, to_b), device_id_type=MESH)
+
+    def hello_row(step, carry):
+        hello(lax.rem(a + step, nx), b)
+        return carry
+
+    lax.fori_loop(1, nx, hello_row, 0)
+    for sx, sy in SIDES:
+        hello(lax.rem(a + sx + nx, nx), lax.rem(b + sy + ny, ny))
+    task_dy, _ = leaf_task(a)
+    leaf_row = jnp.where(task_dy > 0, 1, -1)
+    far_b = lax.rem(b + a - nx // 2 + ny, ny)
+
+    def hello_far(step, carry):
+        to_a = lax.rem(a + step, nx)
+
+        @pl.when((a < 14) & (task_dy != 0))
+        def _():
+            hello(to_a, lax.rem(b + leaf_row + ny, ny))
+
+        @pl.when((to_a != a) | (far_b != b))
+        def _():
+            hello(to_a, far_b)
+
+        return carry
+
+    lax.fori_loop(0, nx, hello_far, 0)
+    for fetch in fetches[:5]:
+        fetch.wait()
+
     for px in range(2):
         for py in range(2):
             cell = halo.at[1 + px, 1 + py]
@@ -102,10 +165,8 @@
                     lane128[0:1] < counts_ref[px, py, k], row, 0.0
                 )
 
-    sides = [(sx, sy) for sx in (-1, 0, 1) for sy in (-1, 0, 1) if (sx, sy) != (0, 0)]
-
     def halo_copy(index):
-        sx, sy = sides[index]
+        sx, sy = SIDES[index]
         src_x = pl.ds(1, 2) if sx == 0 else pl.ds(2 if sx == 1 else 1, 1)
         src_y = pl.ds(1, 2) if sy == 0 else pl.ds(2 if sy == 1 else 1, 1)
         dst_x = pl.ds(1, 2) if sx == 0 else pl.ds(0 if sx == 1 else 3, 1)
@@ -118,9 +179,6 @@
             device_id=(lax.rem(a + sx + nx, nx), lax.rem(b + sy + ny, ny)),
             device_id_type=MESH,
         )
-
-    for index in range(8):
-        halo_copy(index).start()
 
     for chunk in range(8):
         rows = pl.ds(32 * chunk, 32)
@@ -166,6 +224,7 @@
                 weight = turned[:, 12 + k : 13 + k]
                 checks.append(jnp.sum(kernel * weight, axis=0, keepdims=True))
     leaf_check = jnp.concatenate(checks, axis=0)
+    fetches[5].wait()
     leaf_eq = dot_t(leaf_check, cl_up[...])
     for px in range(2):
         for py in range(2):
@@ -207,7 +266,10 @@
 
         return carry
 
+    pl.semaphore_wait(barrier, (nx - 1) + 8 + 12 + jnp.where(a == nx // 2, nx - 1, nx))
     lax.fori_loop(0, nx, leaf_start, 0)
+    for index in range(8):
+        halo_copy(index).start()
 
     eq_hi, eq_lo = split(leaf_eq)
     both = jnp.concatenate([eq_hi, eq_lo], axis=0)
@@ -223,6 +285,7 @@
     check1 = 0.5 * jnp.sum(jnp.where(upper, rows_sum, 0.0), axis=0, keepdims=True)
     row8 = lax.broadcasted_iota(jnp.int32, (8, 256), 0)
     parent_check = jnp.where(row8 == 0, check0, jnp.where(row8 == 1, check1, 0.0))
+    fetches[6].wait()
     par_send[...] = dot_t(parent_check, ct_up[...])
 
     def par_copy(target):
@@ -520,6 +583,8 @@
         for part in range(3):
             sums[part] = sums[part] + rs_recv[source, part]
 
+    fetches[7].wait()
+    fetches[8].wait()
     leaf_local = dot_t(jnp.concatenate([sums[0], sums[1]], axis=0), cl_down[...])
     parent_local = 0.5 * dot_t(sums[2], ct_down[...])
     lanes = lax.broadcasted_iota(jnp.int32, (128, 128), 1)
@@ -579,9 +644,19 @@
     return pl.pallas_call(
         functools.partial(body, nx, ny),
         out_shape=jax.ShapeDtypeStruct(charges.shape, F32),
-        in_specs=[pl.BlockSpec(memory_space=pltpu.SMEM)] + [vmem] * 8,
+        in_specs=[pl.BlockSpec(memory_space=pl.ANY)] * 9,
         out_specs=vmem,
         scratch_shapes=[
+            pltpu.SMEM(counts.shape, jnp.int32),
+            pltpu.VMEM(offsets.shape, F32),
+            pltpu.VMEM(charges.shape, F32),
+            pltpu.VMEM(unit.shape, F32),
+            pltpu.VMEM(unit_t.shape, F32),
+            pltpu.VMEM((256, 256), F32),
+            pltpu.VMEM((256, 256), F32),
+            pltpu.VMEM((256, 256), F32),
+            pltpu.VMEM((256, 256), F32),
+            dma((9,)),
             pltpu.VMEM((4, 4, 16, 128), F32),
             pltpu.VMEM((4, 256, 256), F32),
             pltpu.VMEM((16, 128, 256), F32),
@@ -612,7 +687,7 @@
             dma((nx,)),
         ],
         compiler_params=pltpu.CompilerParams(
-            has_side_effects=True, vmem_limit_bytes=48 * 1024 * 1024
+            has_side_effects=True, collective_id=0, vmem_limit_bytes=56 * 1024 * 1024
         ),
         name="multipole",
     )(counts, offsets, charges, jnp.asarray(unit), jnp.asarray(unit_t), cl_up, cl_down, ct_up, ct_down)

time: 76.4 us -> 62.3 us (0.82)
  Pallas kernels: 67.8 us -> 60.8 us
  local copies, waits for them, and re-layouts: 8.11 us -> 1.3 us
    pallas_call x1, Pallas kernels: 67.8 us -> 60.8 us  [shards(): pl.pallas_call(functools.partial(body, nx, ny), out_shape=jax.ShapeDtypeS...]
    unnamed x19 -> x1, local copies, waits for them, and re-layouts: 8.11 us -> 1.3 us
where the time goes in v2:
time: 62.3 us; the launch traced here: 62.1 us
  Pallas kernels  60.8 us (98%)
  local copies, waits for them, and re-layouts  1.3 us (2%)
    pallas_call x1, Pallas kernels, shards(): pl.pallas_call(functools.partial(body, nx, ny), out_shape=jax.ShapeDtypeS...  60.8 us
    unnamed x1, local copies, waits for them, and re-layouts  1.3 us

profile of v2, /device:TPU:1, one launch (start us, length us, event | category | flops | bytes accessed | tf_op | source)
XLA Modules:
  0.0 62.1 jit_solution(13728621484715092120)
XLA Ops:
  0.0 60.8 %multipole.1 = f32[2,2,4,128]{3,2,1,0:T(4,128)} custom-call(s32[2,2,4]{2,1,0:T(2,128)} %counts_hbm.1, f32[3,2,2,4,128]{4,3,2,1,0:T(4,128)} %off_hbm.1, f32[2,2,4,128]{3,2,1,0:T(4,128)} %chg_hbm.1, f32[8,256]{1,0:T(8,128)} %constant.4.clone.u_hbm, f32[256,8]{1,0:T(8,128)} %constant.5.clone.ut_hbm, f32[256,256]{1,0:T(8,128)} %cl_up_hbm.1, ...), custom_call_target="tpu_custom_call" | custom-call | tf_op jit(solution)/shard_map/multipole/pallas_call | solution.py:644
  60.8 1.3 %copy.11 = f32[2,2,4,128]{3,2,1,0:T(4,128)} copy(f32[2,2,4,128]{3,2,1,0:T(4,128)} %multipole.1) | data formatting | bytes 16384

commit v3 on v2

--- a/solution.py
+++ b/solution.py
@@ -30,6 +30,13 @@
     high = value.astype(BF16)
     low = (value - high.astype(F32)).astype(BF16)
     return high, low
+
+
+def pieces(value):
+    first = value.astype(BF16).astype(F32)
+    rest = value - first
+    second = rest.astype(BF16).astype(F32)
+    return first, second, rest - second
 
 
 def bdot(a, b):
@@ -88,7 +95,14 @@
     l_hi,
     l_lo,
     near_acc,
-    turned_ref,
+    near_lhs,
+    feat,
+    bank_own,
+    bank_x,
+    bank_y,
+    w_own,
+    w_x,
+    w_y,
     halo_ssem,
     halo_rsem,
     leaf_ssem,
@@ -231,46 +245,6 @@
             first = (px * 2 + py) * 4
             leaf_send[py, 4 * px : 4 * px + 4, :] = leaf_eq[first : first + 4, :]
 
-    def leaf_route(target, py):
-        dy, _ = leaf_task(target)
-        src = py + dy
-        valid = (target < 14) & (src >= -2) & (src <= 3)
-        row = (src + 4) // 2 - 2
-        return valid, row, (src + 4) % 2
-
-    def leaf_copy(target, py):
-        valid, row, src_py = leaf_route(target, py)
-        to_b = lax.rem(b - row + ny, ny)
-        copy = pltpu.make_async_remote_copy(
-            src_ref=leaf_send.at[src_py],
-            dst_ref=leaf_recv.at[a, py],
-            send_sem=leaf_ssem.at[target, py],
-            recv_sem=leaf_rsem.at[a, py],
-            device_id=(target, to_b),
-            device_id_type=MESH,
-        )
-        self_copy = (target == a) & (to_b == b)
-        return valid, self_copy, src_py, copy
-
-    def leaf_start(target, carry):
-        for py in range(2):
-            valid, self_copy, src_py, copy = leaf_copy(target, py)
-
-            @pl.when(valid & jnp.logical_not(self_copy))
-            def _():
-                copy.start()
-
-            @pl.when(valid & self_copy)
-            def _():
-                leaf_recv[a, py] = leaf_send[src_py]
-
-        return carry
-
-    pl.semaphore_wait(barrier, (nx - 1) + 8 + 12 + jnp.where(a == nx // 2, nx - 1, nx))
-    lax.fori_loop(0, nx, leaf_start, 0)
-    for index in range(8):
-        halo_copy(index).start()
-
     eq_hi, eq_lo = split(leaf_eq)
     both = jnp.concatenate([eq_hi, eq_lo], axis=0)
     row16 = lax.broadcasted_iota(jnp.int32, (16, 256), 0)
@@ -288,6 +262,138 @@
     fetches[6].wait()
     par_send[...] = dot_t(parent_check, ct_up[...])
 
+    def source_rows(x, y, z):
+        rows = []
+        for value in (x, y, z):
+            q1, q2, q3 = pieces(value)
+            rows += [q1, q2, q1, q2, q3, q1]
+        n1, n2, n3 = pieces((x * x + y * y) + (z * z + SOFT))
+        one = jnp.ones_like(x)
+        return rows + [n1, n2, n3, one, one, one]
+
+    def target_rows(x, y, z):
+        rows = []
+        for value in (x, y, z):
+            p1, p2, p3 = [-2.0 * part for part in pieces(value)]
+            rows += [p1, p1, p2, p2, p1, p3]
+        one = jnp.ones_like(x)
+        n1, n2, n3 = pieces((x * x + y * y) + z * z)
+        return rows + [one, one, one, n1, n2, n3]
+
+    box_row = lax.broadcasted_iota(jnp.int32, (16, 128), 0)
+    own_x, own_y, own_z, own_w = [
+        jnp.concatenate(
+            [halo[1 + px, 1 + py, 4 * comp : 4 * comp + 4, :] for px in (0, 1) for py in (0, 1)],
+            axis=0,
+        )
+        for comp in range(4)
+    ]
+    own_x = own_x + ((box_row // 8) - 1).astype(F32)
+    own_y = own_y + ((box_row // 4 % 2) - 1).astype(F32)
+    own_z = own_z - 0.5
+    feat[pl.ds(384, 128), :] = jnp.zeros((128, 128), F32)
+    for index, value in enumerate(source_rows(own_x, own_y, own_z)):
+        feat[16 * index : 16 * index + 16, :] = value
+    for column in range(4):
+        for layer in range(4):
+            block = feat[pl.ds(4 * column + layer, 32, stride=16), :]
+            bank_own[layer, :, 128 * column : 128 * column + 128] = block.astype(BF16)
+            row = own_w[4 * column + layer : 4 * column + layer + 1, :]
+            w_own[layer, 0:1, 128 * column : 128 * column + 128] = row
+    for turn in range(3):
+        for index, value in enumerate(target_rows(own_x, own_y, own_z - float(turn - 1))):
+            feat[16 * index : 16 * index + 16, :] = value
+        for box in range(16):
+            block = feat[pl.ds(box, 32, stride=16), :]
+            near_lhs[turn, box] = jnp.transpose(block).astype(BF16)
+
+    lane512 = lax.broadcasted_iota(jnp.int32, (128, 512), 1)
+    row512 = lax.broadcasted_iota(jnp.int32, (128, 512), 0)
+
+    def fold(value):
+        total = value[:, 0:128]
+        for first in range(128, value.shape[1], 128):
+            total = total + value[:, first : first + 128]
+        return total
+
+    def near_own(turn):
+        low = max(0, 1 - turn)
+        count = 4 - abs(turn - 1)
+
+        def step(index, carry):
+            column = index // count
+            layer = index % count + low
+            box = 4 * column + layer
+            source = layer + turn - 1
+            kernel = lax.rsqrt(bdot(near_lhs[turn, box], bank_own[source]))
+            if turn == 1:
+                kernel = jnp.where(lane512 == row512 + 128 * column, 0.0, kernel)
+            value = fold(kernel * w_own[source, 0:1, :])
+            near_acc[box] = value if turn == 1 else near_acc[box] + value
+            return carry
+
+        lax.fori_loop(0, 4 * count, step, 0)
+
+    def near_halo(turn):
+        low = max(0, 1 - turn)
+        count = 4 - abs(turn - 1)
+
+        def step(index, carry):
+            column = index // count
+            layer = index % count + low
+            box = 4 * column + layer
+            source = layer + turn - 1
+            px = column // 2
+            py = column % 2
+            lanes = pl.ds(pl.multiple_of(128 * py, 128), 384)
+            lhs = near_lhs[turn, box]
+            value = lax.rsqrt(bdot(lhs, bank_x[source, px, :, lanes]))
+            value = fold(value * w_x[source, px, 0:1, lanes])
+            other = lax.rsqrt(bdot(lhs, bank_y[source, py]))
+            other = fold(other * w_y[source, py, 0:1, :])
+            near_acc[box] = near_acc[box] + (value + other)
+            return carry
+
+        lax.fori_loop(0, 4 * count, step, 0)
+
+    for turn in (1, 0, 2):
+        near_own(turn)
+
+    def leaf_route(target, py):
+        dy, _ = leaf_task(target)
+        src = py + dy
+        valid = (target < 14) & (src >= -2) & (src <= 3)
+        row = (src + 4) // 2 - 2
+        return valid, row, (src + 4) % 2
+
+    def leaf_copy(target, py):
+        valid, row, src_py = leaf_route(target, py)
+        to_b = lax.rem(b - row + ny, ny)
+        copy = pltpu.make_async_remote_copy(
+            src_ref=leaf_send.at[src_py],
+            dst_ref=leaf_recv.at[a, py],
+            send_sem=leaf_ssem.at[target, py],
+            recv_sem=leaf_rsem.at[a, py],
+            device_id=(target, to_b),
+            device_id_type=MESH,
+        )
+        self_copy = (target == a) & (to_b == b)
+        return valid, self_copy, src_py, copy
+
+    def leaf_start(target, carry):
+        for py in range(2):
+            valid, self_copy, src_py, copy = leaf_copy(target, py)
+
+            @pl.when(valid & jnp.logical_not(self_copy))
+            def _():
+                copy.start()
+
+            @pl.when(valid & self_copy)
+            def _():
+                leaf_recv[a, py] = leaf_send[src_py]
+
+        return carry
+
     def par_copy(target):
         to_b = lax.rem(b - target + nx // 2 + ny, ny)
         copy = pltpu.make_async_remote_copy(
@@ -313,55 +419,12 @@
 
         return carry
 
+    pl.semaphore_wait(barrier, (nx - 1) + 8 + 12 + jnp.where(a == nx // 2, nx - 1, nx))
+    lax.fori_loop(0, nx, leaf_start, 0)
+    for index in range(8):
+        halo_copy(index).start()
+
     lax.fori_loop(0, nx, par_start, 0)
-
-    sub8 = lax.broadcasted_iota(jnp.int32, (8, 128), 0)
-    lane8 = lax.broadcasted_iota(jnp.int32, (8, 128), 1)
-
-    def near_column(fx, fy):
-        turned_ref[...] = jnp.transpose(halo[fx, fy])
-        columns = [
-            (px, py)
-            for px in range(2)
-            for py in range(2)
-            if abs(px + 1 - fx) <= 1 and abs(py + 1 - fy) <= 1
-        ]
-        pairs = [(px, py, k) for px, py in columns for k in range(4)]
-
-        def tile(t, carry):
-            sums = list(carry)
-            block = turned_ref[pl.ds(pl.multiple_of(8 * t, 8), 8), :]
-            for ks in range(4):
-                source = [
-                    jnp.broadcast_to(block[:, 4 * comp + ks : 4 * comp + ks + 1], (8, 128))
-                    for comp in range(4)
-                ]
-                for slot, (px, py, k) in enumerate(pairs):
-                    if abs(k - ks) > 1:
-                        continue
-                    shift = (px + 1 - fx, py + 1 - fy, k - ks)
-                    total = None
-                    for comp in range(3):
-                        row = halo[1 + px, 1 + py, 4 * comp + k : 4 * comp + k + 1, :]
-                        if shift[comp]:
-                            row = row + float(shift[comp])
-                        diff = row - source[comp]
-                        total = diff * diff + SOFT if total is None else total + diff * diff
-                    kernel = lax.rsqrt(total)
-                    if shift == (0, 0, 0):
-                        kernel = jnp.where(lane8 == sub8 + 8 * t, 0.0, kernel)
-                    sums[slot] = sums[slot] + kernel * source[3]
-            return tuple(sums)
-
-        start = tuple(near_acc[(px * 2 + py) * 4 + k] for px, py, k in pairs)
-        done = lax.fori_loop(0, 16, tile, start)
-        for slot, (px, py, k) in enumerate(pairs):
-            near_acc[(px * 2 + py) * 4 + k] = done[slot]
-
-    near_acc[...] = jnp.zeros_like(near_acc)
-    for fx in (1, 2):
-        for fy in (1, 2):
-            near_column(fx, fy)
 
     for px in range(2):
         for py in range(2):
@@ -560,10 +623,40 @@
 
     for index in range(8):
         halo_copy(7 - index).wait_recv()
-    for fx in range(4):
-        for fy in range(4):
-            if fx in (0, 3) or fy in (0, 3):
-                near_column(fx, fy)
+    for strip in range(4):
+        if strip < 2:
+            cells = [(3 * strip, fy) for fy in range(4)]
+        else:
+            cells = [(1, 3 * (strip - 2)), (2, 3 * (strip - 2))]
+        side_x, side_y, side_z, side_w = [
+            jnp.concatenate(
+                [halo[fx, fy, 4 * comp : 4 * comp + 4, :] for fx, fy in cells], axis=0
+            )
+            for comp in range(4)
+        ]
+        size = 4 * len(cells)
+        place = lax.broadcasted_iota(jnp.int32, (size, 128), 0) // 4
+        if strip < 2:
+            side_x = side_x + float(3 * strip - 2)
+            side_y = side_y + (place - 2).astype(F32)
+        else:
+            side_x = side_x + (place - 1).astype(F32)
+            side_y = side_y + float(3 * (strip - 2) - 2)
+        for index, value in enumerate(source_rows(side_x, side_y, side_z - 0.5)):
+            feat[size * index : size * index + size, :] = value
+        feat[pl.ds(24 * size, 8 * size), :] = jnp.zeros((8 * size, 128), F32)
+        for cell in range(len(cells)):
+            for layer in range(4):
+                block = feat[pl.ds(4 * cell + layer, 32, stride=size), :].astype(BF16)
+                row = side_w[4 * cell + layer : 4 * cell + layer + 1, :]
+                if strip < 2:
+                    bank_x[layer, strip, :, 128 * cell : 128 * cell + 128] = block
+                    w_x[layer, strip, 0:1, 128 * cell : 128 * cell + 128] = row
+                else:
+                    bank_y[layer, strip - 2, :, 128 * cell : 128 * cell + 128] = block
+                    w_y[layer, strip - 2, 0:1, 128 * cell : 128 * cell + 128] = row
+    for turn in (1, 0, 2):
+        near_halo(turn)
 
     def rs_wait(step, carry):
         source = lax.rem(a + step, nx)
@@ -593,6 +686,7 @@
         layer = (box % 4) // 2
         value = k_leaf[box] * leaf_local[box : box + 1, :]
         value = value + k_parent[box] * parent_local[layer : layer + 1, :]
+        value = value[:, :128] + value[:, 128:] + near_acc[box]
         column = jnp.sum(value, axis=1, keepdims=True)
         columns = jnp.where(lanes == box, column, columns)
     flipped = jnp.transpose(columns)
@@ -600,7 +694,7 @@
         for py in range(2):
             for k in range(4):
                 box = (px * 2 + py) * 4 + k
-                row = flipped[box : box + 1, :] + jnp.sum(near_acc[box], axis=0, keepdims=True)
+                row = flipped[box : box + 1, :]
                 out_ref[px, py, k : k + 1, :] = jnp.where(
                     lane128[0:1] < counts_ref[px, py, k], row, 0.0
                 )
@@ -675,8 +769,15 @@
             pltpu.VMEM((7, 256, 256), BF16),
             pltpu.VMEM((6, 8 * nx, 256), BF16),
             pltpu.VMEM((6, 8 * nx, 256), BF16),
-            pltpu.VMEM((16, 8, 128), F32),
-            pltpu.VMEM((128, 16), F32),
+            pltpu.VMEM((16, 128, 128), F32),
+            pltpu.VMEM((3, 16, 128, 32), BF16),
+            pltpu.VMEM((512, 128), F32),
+            pltpu.VMEM((4, 32, 512), BF16),
+            pltpu.VMEM((4, 2, 32, 512), BF16),
+            pltpu.VMEM((4, 2, 32, 256), BF16),
+            pltpu.VMEM((4, 8, 512), F32),
+            pltpu.VMEM((4, 2, 8, 512), F32),
+            pltpu.VMEM((4, 2, 8, 256), F32),
             dma((8,)),
             dma((8,)),
             dma((nx, 2)),

time: 62.3 us -> 54.4 us (0.87)
  Pallas kernels: 60.8 us -> 53 us
    pallas_call x1, Pallas kernels: 60.8 us -> 53 us  [shards(): pl.pallas_call(functools.partial(body, nx, ny), out_shape=jax.ShapeDtypeS...]
where the time goes in v3:
time: 54.4 us; the launch traced here: 54.3 us
  Pallas kernels  53 us (97%)
  local copies, waits for them, and re-layouts  1.3 us (2%)
    pallas_call x1, Pallas kernels, shards(): pl.pallas_call(functools.partial(body, nx, ny), out_shape=jax.ShapeDtypeS...  53 us
    unnamed x1, local copies, waits for them, and re-layouts  1.3 us

profile of v3, /device:TPU:1, one launch (start us, length us, event | category | flops | bytes accessed | tf_op | source)
XLA Modules:
  0.0 54.3 jit_solution(6494933951301621457)
XLA Ops:
  0.0 53.0 %multipole.1 = f32[2,2,4,128]{3,2,1,0:T(4,128)} custom-call(s32[2,2,4]{2,1,0:T(2,128)} %counts_hbm.1, f32[3,2,2,4,128]{4,3,2,1,0:T(4,128)} %off_hbm.1, f32[2,2,4,128]{3,2,1,0:T(4,128)} %chg_hbm.1, f32[8,256]{1,0:T(8,128)} %constant.4.clone.u_hbm, f32[256,8]{1,0:T(8,128)} %constant.5.clone.ut_hbm, f32[256,256]{1,0:T(8,128)} %cl_up_hbm.1, ...), custom_call_target="tpu_custom_call" | custom-call | tf_op jit(solution)/shard_map/multipole/pallas_call | solution.py:738
  53.0 1.3 %copy.11 = f32[2,2,4,128]{3,2,1,0:T(4,128)} copy(f32[2,2,4,128]{3,2,1,0:T(4,128)} %multipole.1) | data formatting | bytes 16384

commit v4 on v3

--- a/solution.py
+++ b/solution.py
@@ -260,7 +260,7 @@
     row8 = lax.broadcasted_iota(jnp.int32, (8, 256), 0)
     parent_check = jnp.where(row8 == 0, check0, jnp.where(row8 == 1, check1, 0.0))
     fetches[6].wait()
-    par_send[...] = dot_t(parent_check, ct_up[...])
+    par_send[...] = dot_t(parent_check, ct_up[...])[0:2]
 
     def source_rows(x, y, z):
         rows = []
@@ -356,9 +356,6 @@
 
         lax.fori_loop(0, 4 * count, step, 0)
 
-    for turn in (1, 0, 2):
-        near_own(turn)
-
     def leaf_route(target, py):
         dy, _ = leaf_task(target)
         src = py + dy
@@ -419,13 +416,6 @@
 
         return carry
 
-    pl.semaphore_wait(barrier, (nx - 1) + 8 + 12 + jnp.where(a == nx // 2, nx - 1, nx))
-    lax.fori_loop(0, nx, leaf_start, 0)
-    for index in range(8):
-        halo_copy(index).start()
-
-    lax.fori_loop(0, nx, par_start, 0)
-
     for px in range(2):
         for py in range(2):
             turned = jnp.transpose(halo[1 + px, 1 + py])
@@ -437,6 +427,15 @@
                     diff = centre[comp] - place
                     total = total + diff * diff
                 k_parent[box] = lax.rsqrt(total)
+
+    pl.semaphore_wait(barrier, (nx - 1) + 8 + 12 + jnp.where(a == nx // 2, nx - 1, nx))
+    lax.fori_loop(0, nx, par_start, 0)
+    lax.fori_loop(0, nx, leaf_start, 0)
+    for index in range(8):
+        halo_copy(index).start()
+
+    for turn in (1, 0, 2):
+        near_own(turn)
 
     def par_wait(source, carry):
         from_b = lax.rem(b + a - nx // 2 + ny, ny)
@@ -759,8 +758,8 @@
             pltpu.VMEM((8, 256, 256), BF16),
             pltpu.VMEM((2, 8, 256), F32),
             pltpu.VMEM((nx, 2, 8, 256), F32),
-            pltpu.VMEM((8, 256), F32),
-            pltpu.VMEM((nx, 8, 256), F32),
+            pltpu.VMEM((2, 256), F32),
+            pltpu.VMEM((nx, 2, 256), F32),
             pltpu.VMEM((nx, 3, 8, 256), F32),
             pltpu.VMEM((nx, 3, 8, 256), F32),
             pltpu.VMEM((2, 8 * nx, 256), F32),

time: 54.4 us -> 45.5 us (0.84)
  Pallas kernels: 53 us -> 44.1 us
    pallas_call x1, Pallas kernels: 53 us -> 44.1 us  [shards(): pl.pallas_call(functools.partial(body, nx, ny), out_shape=jax.ShapeDtypeS...]
where the time goes in v4:
time: 45.5 us; the launch traced here: 45.4 us
  Pallas kernels  44.1 us (97%)
  local copies, waits for them, and re-layouts  1.3 us (3%)
    pallas_call x1, Pallas kernels, shards(): pl.pallas_call(functools.partial(body, nx, ny), out_shape=jax.ShapeDtypeS...  44.1 us
    unnamed x1, local copies, waits for them, and re-layouts  1.3 us

profile of v4, /device:TPU:1, one launch (start us, length us, event | category | flops | bytes accessed | tf_op | source)
XLA Modules:
  0.0 45.4 jit_solution(17785421597466184035)
XLA Ops:
  0.0 44.1 %multipole.1 = f32[2,2,4,128]{3,2,1,0:T(4,128)} custom-call(s32[2,2,4]{2,1,0:T(2,128)} %counts_hbm.1, f32[3,2,2,4,128]{4,3,2,1,0:T(4,128)} %off_hbm.1, f32[2,2,4,128]{3,2,1,0:T(4,128)} %chg_hbm.1, f32[8,256]{1,0:T(8,128)} %constant.4.clone.u_hbm, f32[256,8]{1,0:T(8,128)} %constant.5.clone.ut_hbm, f32[256,256]{1,0:T(8,128)} %cl_up_hbm.1, ...), custom_call_target="tpu_custom_call" | custom-call | tf_op jit(solution)/shard_map/multipole/pallas_call | solution.py:737
  44.1 1.3 %copy.11 = f32[2,2,4,128]{3,2,1,0:T(4,128)} copy(f32[2,2,4,128]{3,2,1,0:T(4,128)} %multipole.1) | data formatting | bytes 16384

commit v5 on v4

--- a/solution.py
+++ b/solution.py
@@ -92,8 +92,9 @@
     par_ring,
     m_hi,
     m_lo,
-    l_hi,
-    l_lo,
+    l_three,
+    m_three,
+    lines,
     near_acc,
     near_lhs,
     feat,
@@ -201,6 +202,9 @@
             diff = 0.9 * (u_ref[comp : comp + 1, :] - ut_ref[rows, comp : comp + 1])
             tables[1 + comp, rows, :] = -2.0 * diff
             total = total + diff * diff
+            if comp == 0:
+                for dx in (-3, -2, -1, 1, 2, 3):
+                    lines[dx + 3, rows, :] = (-2.0 * dx) * diff + float(dx * dx)
         tables[0, rows, :] = total
 
     def child_chunk(chunk, carry):
@@ -318,43 +322,39 @@
 
     def near_own(turn):
         low = max(0, 1 - turn)
-        count = 4 - abs(turn - 1)
-
-        def step(index, carry):
-            column = index // count
-            layer = index % count + low
-            box = 4 * column + layer
+
+        def step(layer, carry):
             source = layer + turn - 1
-            kernel = lax.rsqrt(bdot(near_lhs[turn, box], bank_own[source]))
-            if turn == 1:
-                kernel = jnp.where(lane512 == row512 + 128 * column, 0.0, kernel)
-            value = fold(kernel * w_own[source, 0:1, :])
-            near_acc[box] = value if turn == 1 else near_acc[box] + value
+            for column in range(4):
+                box = 4 * column + layer
+                kernel = lax.rsqrt(bdot(near_lhs[turn, box], bank_own[source]))
+                if turn == 1:
+                    kernel = jnp.where(lane512 == row512 + 128 * column, 0.0, kernel)
+                value = fold(kernel * w_own[source, 0:1, :])
+                near_acc[box] = value if turn == 1 else near_acc[box] + value
             return carry
 
-        lax.fori_loop(0, 4 * count, step, 0)
+        lax.fori_loop(low, low + 4 - abs(turn - 1), step, 0)
 
     def near_halo(turn):
         low = max(0, 1 - turn)
-        count = 4 - abs(turn - 1)
-
-        def step(index, carry):
-            column = index // count
-            layer = index % count + low
-            box = 4 * column + layer
+
+        def step(layer, carry):
             source = layer + turn - 1
-            px = column // 2
-            py = column % 2
-            lanes = pl.ds(pl.multiple_of(128 * py, 128), 384)
-            lhs = near_lhs[turn, box]
-            value = lax.rsqrt(bdot(lhs, bank_x[source, px, :, lanes]))
-            value = fold(value * w_x[source, px, 0:1, lanes])
-            other = lax.rsqrt(bdot(lhs, bank_y[source, py]))
-            other = fold(other * w_y[source, py, 0:1, :])
-            near_acc[box] = near_acc[box] + (value + other)
+            for column in range(4):
+                box = 4 * column + layer
+                px = column // 2
+                py = column % 2
+                lanes = pl.ds(128 * py, 384)
+                lhs = near_lhs[turn, box]
+                value = lax.rsqrt(bdot(lhs, bank_x[source, px, :, lanes]))
+                value = fold(value * w_x[source, px, 0:1, lanes])
+                other = lax.rsqrt(bdot(lhs, bank_y[source, py]))
+                other = fold(other * w_y[source, py, 0:1, :])
+                near_acc[box] = near_acc[box] + (value + other)
             return carry
 
-        lax.fori_loop(0, 4 * count, step, 0)
+        lax.fori_loop(low, low + 4 - abs(turn - 1), step, 0)
 
     def leaf_route(target, py):
         dy, _ = leaf_task(target)
@@ -463,38 +463,46 @@
     oy = a - nx // 2
     oy_f = oy.astype(F32)
 
-    def far_step(index, carry):
-        acc0, acc1 = carry
+    for chunk in range(8):
+        rows = pl.ds(32 * chunk, 32)
+        lines[7, rows, :] = tables[0, rows, :] + (
+            oy_f * tables[2, rows, :] + (oy_f * oy_f + SOFT / 4)
+        )
+
+    def far_offset(index, first_slot, acc0, acc1):
         ox = index - nx // 2
         ox_f = ox.astype(F32)
         keep = (ox > 1) | (ox < -1) | (oy > 1) | (oy < -1)
-        const = ox_f * ox_f + oy_f * oy_f + SOFT / 4
         for chunk in range(8):
             rows = pl.ds(32 * chunk, 32)
-            flat = tables[0, rows, :] + ox_f * tables[1, rows, :] + oy_f * tables[2, rows, :]
-            flat = flat + const
+            flat = lines[7, rows, :] + (ox_f * tables[1, rows, :] + ox_f * ox_f)
+            tall = flat + 1.0
             lift = tables[3, rows, :]
-            for slot, value in enumerate((flat + 1.0 - lift, flat, flat + 1.0 + lift)):
-                high, low = split(jnp.where(keep, lax.rsqrt(value), 0.0))
-                m_hi[slot, rows, :] = high
-                m_lo[slot, rows, :] = low
+            for slot, value in enumerate((tall - lift, flat, tall + lift)):
+                high, low = split(lax.rsqrt(value))
+                m_hi[first_slot + slot, rows, :] = high
+                m_lo[first_slot + slot, rows, :] = low
         turn = lax.rem(nx + nx // 2 - index, nx)
-        p0h, p0l = split(pltpu.roll(par_ring[0], turn, 0))
-        p1h, p1l = split(pltpu.roll(par_ring[1], turn, 0))
-        same = bdot(jnp.concatenate([p0h, p1h, p0l, p1l], axis=0), m_hi[1])
-        same2 = bdot(jnp.concatenate([p0h, p1h], axis=0), m_lo[1])
-        up = bdot(jnp.concatenate([p1h, p1l], axis=0), m_hi[2])
-        up2 = bdot(p1h, m_lo[2])
-        down = bdot(jnp.concatenate([p0h, p0l], axis=0), m_hi[0])
-        down2 = bdot(p0h, m_lo[0])
+        p0h, p0l = split(jnp.where(keep, pltpu.roll(par_ring[0], turn, 0), 0.0))
+        p1h, p1l = split(jnp.where(keep, pltpu.roll(par_ring[1], turn, 0), 0.0))
+        same = bdot(jnp.concatenate([p0h, p1h, p0l, p1l], axis=0), m_hi[first_slot + 1])
+        same2 = bdot(jnp.concatenate([p0h, p1h], axis=0), m_lo[first_slot + 1])
+        up = bdot(jnp.concatenate([p1h, p1l], axis=0), m_hi[first_slot + 2])
+        up2 = bdot(p1h, m_lo[first_slot + 2])
+        down = bdot(jnp.concatenate([p0h, p0l], axis=0), m_hi[first_slot])
+        down2 = bdot(p0h, m_lo[first_slot])
         acc0 = acc0 + ((same[0:16] + up[0:16]) + (same[32:48] + same2[0:16] + up[16:32] + up2))
         acc1 = acc1 + (
             (same[16:32] + down[0:16]) + (same[48:64] + same2[16:32] + down[16:32] + down2)
         )
         return acc0, acc1
 
+    def far_step(index, carry):
+        carry = far_offset(2 * index, 0, *carry)
+        return far_offset(2 * index + 1, 3, *carry)
+
     zero16 = jnp.zeros((16, 256), F32)
-    far0, far1 = lax.fori_loop(0, nx, far_step, (zero16, zero16))
+    far0, far1 = lax.fori_loop(0, nx // 2, far_step, (zero16, zero16))
     for target in range(nx):
         rs_send[target, 2] = jnp.where(
             row8 == 0,
@@ -559,21 +567,6 @@
             def _():
                 dz_f = dz.astype(F32)
                 beside = (dy >= -1) & (dy <= 1) & (dz >= -1) & (dz <= 1)
-                const = dy_f * dy_f + dz_f * dz_f + SOFT
-                for chunk in range(8):
-                    rows = pl.ds(32 * chunk, 32)
-                    base = tables[0, rows, :] + dy_f * tables[2, rows, :]
-                    base = base + dz_f * tables[3, rows, :] + const
-                    along = tables[1, rows, :]
-                    for slot in range(7):
-                        dx = slot - 3
-                        value = base + (float(dx) * along + float(dx * dx)) if dx else base
-                        kernel = lax.rsqrt(value)
-                        if abs(dx) <= 1:
-                            kernel = jnp.where(beside, 0.0, kernel)
-                        high, low = split(kernel)
-                        m_hi[slot, rows, :] = high
-                        m_lo[slot, rows, :] = low
                 inside = (row128 + dz >= 0) & (row128 + dz <= 3)
                 turn = lax.rem(128 - dz, 128)
                 for sx in range(2):
@@ -587,17 +580,35 @@
                             placed = moved
                         slot = 2 * block + sx + 2
                         high, low = split(placed)
-                        l_hi[slot] = high
-                        l_lo[slot] = low
+                        l_three[slot, :, 0:256] = high
+                        l_three[slot, :, 256:512] = low
+                        l_three[slot, :, 512:768] = high
+                const = dy_f * dy_f + dz_f * dz_f + SOFT
+                for chunk in range(8):
+                    rows = pl.ds(32 * chunk, 32)
+                    base = tables[0, rows, :] + dy_f * tables[2, rows, :]
+                    lines[7, rows, :] = base + (dz_f * tables[3, rows, :] + const)
+                totals = [rs_send[:, px].reshape(8 * nx, 256) for px in range(2)]
+                for matrix in range(7):
+                    dx = matrix - 3
+                    for chunk in range(8):
+                        rows = pl.ds(32 * chunk, 32)
+                        value = lines[7, rows, :]
+                        if dx:
+                            value = value + lines[matrix, rows, :]
+                        kernel = lax.rsqrt(value)
+                        if abs(dx) <= 1:
+                            kernel = jnp.where(beside, 0.0, kernel)
+                        high, low = split(kernel)
+                        m_three[matrix, 32 * chunk : 32 * chunk + 32, :] = high
+                        m_three[matrix, 256 + 32 * chunk : 288 + 32 * chunk, :] = high
+                        m_three[matrix, 512 + 32 * chunk : 544 + 32 * chunk, :] = low
+                    for px in range(2):
+                        slot = matrix - 1 + px
+                        if 0 <= slot < 6:
+                            totals[px] = totals[px] + bdot(l_three[slot], m_three[matrix])
                 for px in range(2):
-                    total = jnp.zeros((128, 256), F32)
-                    for slot in range(6):
-                        matrix = slot + 1 - px
-                        total = total + (
-                            bdot(l_hi[slot], m_hi[matrix])
-                            + (bdot(l_lo[slot], m_hi[matrix]) + bdot(l_hi[slot], m_lo[matrix]))
-                        )
-                    rs_send[:, px] = rs_send[:, px] + total.reshape(nx, 8, 256)
+                    rs_send[:, px] = totals[px].reshape(nx, 8, 256)
 
             return carry
 
@@ -764,10 +775,11 @@
             pltpu.VMEM((nx, 3, 8, 256), F32),
             pltpu.VMEM((2, 8 * nx, 256), F32),
             pltpu.VMEM((2, nx, 256), F32),
-            pltpu.VMEM((7, 256, 256), BF16),
-            pltpu.VMEM((7, 256, 256), BF16),
-            pltpu.VMEM((6, 8 * nx, 256), BF16),
-            pltpu.VMEM((6, 8 * nx, 256), BF16),
+            pltpu.VMEM((6, 256, 256), BF16),
+            pltpu.VMEM((6, 256, 256), BF16),
+            pltpu.VMEM((6, 8 * nx, 768), BF16),
+            pltpu.VMEM((7, 768, 256), BF16),
+            pltpu.VMEM((8, 256, 256), F32),
             pltpu.VMEM((16, 128, 128), F32),
             pltpu.VMEM((3, 16, 128, 32), BF16),
             pltpu.VMEM((512, 128), F32),

time: 45.5 us -> 39.7 us (0.87)
  the two profiles are of different devices: /device:TPU:1 before, /device:TPU:27 now
where the time goes in v5:
time: 39.7 us; the launch traced here: 39.5 us
  Pallas kernels  38.2 us (96%)
  local copies, waits for them, and re-layouts  1.3 us (3%)
    pallas_call x1, Pallas kernels, shards(): pl.pallas_call(functools.partial(body, nx, ny), out_shape=jax.ShapeDtypeS...  38.2 us
    unnamed x1, local copies, waits for them, and re-layouts  1.3 us

profile of v5, /device:TPU:27, one launch (start us, length us, event | category | flops | bytes accessed | tf_op | source)
XLA Modules:
  0.0 39.5 jit_solution(4953262656047695013)
XLA Ops:
  0.0 38.2 %multipole.1 = f32[2,2,4,128]{3,2,1,0:T(4,128)} custom-call(s32[2,2,4]{2,1,0:T(2,128)} %counts_hbm.1, f32[3,2,2,4,128]{4,3,2,1,0:T(4,128)} %off_hbm.1, f32[2,2,4,128]{3,2,1,0:T(4,128)} %chg_hbm.1, f32[8,256]{1,0:T(8,128)} %constant.4.clone.u_hbm, f32[256,8]{1,0:T(8,128)} %constant.5.clone.ut_hbm, f32[256,256]{1,0:T(8,128)} %cl_up_hbm.1, ...), custom_call_target="tpu_custom_call" | custom-call | tf_op jit(solution)/shard_map/multipole/pallas_call | solution.py:748
  38.2 1.3 %copy.11 = f32[2,2,4,128]{3,2,1,0:T(4,128)} copy(f32[2,2,4,128]{3,2,1,0:T(4,128)} %multipole.1) | data formatting | bytes 16384

commit v6 on v5

--- a/solution.py
+++ b/solution.py
@@ -11,7 +11,6 @@
 SOFT = 0.0004
 F32 = jnp.float32
 BF16 = jnp.bfloat16
-HIGHEST = lax.Precision.HIGHEST
 MESH = pl.DeviceIdType.MESH
 SIDES = [(sx, sy) for sx in (-1, 0, 1) for sy in (-1, 0, 1) if (sx, sy) != (0, 0)]
 
@@ -43,10 +42,10 @@
     return jnp.dot(a, b, preferred_element_type=F32)
 
 
-def dot_t(a, b):
-    return lax.dot_general(
-        a, b, (((1,), (1,)), ((), ())), precision=HIGHEST, preferred_element_type=F32
-    )
+def wrap(value, size):
+    if size & (size - 1) == 0:
+        return value & (size - 1)
+    return lax.rem(value + size, size)
 
 
 def leaf_task(a):
@@ -96,6 +95,8 @@
     m_three,
     lines,
     near_acc,
+    op_hi,
+    op_lo,
     near_lhs,
     feat,
     bank_own,
@@ -117,6 +118,37 @@
     b = lax.axis_index("gy")
     lane128 = lax.broadcasted_iota(jnp.int32, (4, 128), 1)
 
+    barrier = pltpu.get_barrier_semaphore()
+
+    def hello(to_a, to_b):
+        pl.semaphore_signal(barrier, inc=1, device_id=(to_a, to_b), device_id_type=MESH)
+
+    def hello_row(step, carry):
+        hello(wrap(a + step, nx), b)
+        return carry
+
+    lax.fori_loop(1, nx, hello_row, 0)
+    for sx, sy in SIDES:
+        hello(wrap(a + sx, nx), wrap(b + sy, ny))
+    task_dy, _ = leaf_task(a)
+    leaf_row = jnp.where(task_dy > 0, 1, -1)
+    far_b = wrap(b + a - nx // 2, ny)
+    leaf_b = wrap(b + leaf_row, ny)
+
+    def hello_far(step, carry):
+        to_a = wrap(a + step, nx)
+
+        @pl.when((a < 14) & (task_dy != 0))
+        def _():
+            hello(to_a, leaf_b)
+
+        @pl.when((to_a != a) | (far_b != b))
+        def _():
+            hello(to_a, far_b)
+
+        return carry
+
+    lax.fori_loop(0, nx, hello_far, 0)
     fetches = [
         pltpu.make_async_copy(src, dst, in_sem.at[index])
         for index, (src, dst) in enumerate(
@@ -135,37 +167,6 @@
     ]
     for fetch in fetches:
         fetch.start()
-
-    barrier = pltpu.get_barrier_semaphore()
-
-    def hello(to_a, to_b):
-        pl.semaphore_signal(barrier, inc=1, device_id=(to_a, to_b), device_id_type=MESH)
-
-    def hello_row(step, carry):
-        hello(lax.rem(a + step, nx), b)
-        return carry
-
-    lax.fori_loop(1, nx, hello_row, 0)
-    for sx, sy in SIDES:
-        hello(lax.rem(a + sx + nx, nx), lax.rem(b + sy + ny, ny))
-    task_dy, _ = leaf_task(a)
-    leaf_row = jnp.where(task_dy > 0, 1, -1)
-    far_b = lax.rem(b + a - nx // 2 + ny, ny)
-
-    def hello_far(step, carry):
-        to_a = lax.rem(a + step, nx)
-
-        @pl.when((a < 14) & (task_dy != 0))
-        def _():
-            hello(to_a, lax.rem(b + leaf_row + ny, ny))
-
-        @pl.when((to_a != a) | (far_b != b))
-        def _():
-            hello(to_a, far_b)
-
-        return carry
-
-    lax.fori_loop(0, nx, hello_far, 0)
     for fetch in fetches[:5]:
         fetch.wait()
 
@@ -191,21 +192,9 @@
             dst_ref=halo.at[dst_x, dst_y],
             send_sem=halo_ssem.at[index],
             recv_sem=halo_rsem.at[index],
-            device_id=(lax.rem(a + sx + nx, nx), lax.rem(b + sy + ny, ny)),
+            device_id=(wrap(a + sx, nx), wrap(b + sy, ny)),
             device_id_type=MESH,
         )
-
-    for chunk in range(8):
-        rows = pl.ds(32 * chunk, 32)
-        total = jnp.zeros((32, 256), F32)
-        for comp in range(3):
-            diff = 0.9 * (u_ref[comp : comp + 1, :] - ut_ref[rows, comp : comp + 1])
-            tables[1 + comp, rows, :] = -2.0 * diff
-            total = total + diff * diff
-            if comp == 0:
-                for dx in (-3, -2, -1, 1, 2, 3):
-                    lines[dx + 3, rows, :] = (-2.0 * dx) * diff + float(dx * dx)
-        tables[0, rows, :] = total
 
     def child_chunk(chunk, carry):
         rows = pl.ds(pl.multiple_of(32 * chunk, 32), 32)
@@ -225,6 +214,19 @@
         return carry
 
     lax.fori_loop(0, 8, child_chunk, 0)
+
+    def prepare(matrix, slot):
+        high, low = split(jnp.transpose(matrix[...]))
+        op_hi[slot] = high
+        op_lo[slot] = low
+
+    def apply(rows, slot):
+        if rows.shape[0] < 16:
+            rows = jnp.concatenate([rows, jnp.zeros((16 - rows.shape[0], 256), F32)], axis=0)
+        high, low = split(rows)
+        first = bdot(jnp.concatenate([high, low], axis=0), op_hi[slot])
+        count = rows.shape[0]
+        return first[:count] + (first[count:] + bdot(high, op_lo[slot]))
 
     centre = [0.5 + 1.8 * u_ref[comp : comp + 1, :] for comp in range(3)]
     checks = []
@@ -243,7 +245,10 @@
                 checks.append(jnp.sum(kernel * weight, axis=0, keepdims=True))
     leaf_check = jnp.concatenate(checks, axis=0)
     fetches[5].wait()
-    leaf_eq = dot_t(leaf_check, cl_up[...])
+    fetches[6].wait()
+    prepare(cl_up, 0)
+    prepare(ct_up, 1)
+    leaf_eq = apply(leaf_check, 0)
     for px in range(2):
         for py in range(2):
             first = (px * 2 + py) * 4
@@ -263,8 +268,97 @@
     check1 = 0.5 * jnp.sum(jnp.where(upper, rows_sum, 0.0), axis=0, keepdims=True)
     row8 = lax.broadcasted_iota(jnp.int32, (8, 256), 0)
     parent_check = jnp.where(row8 == 0, check0, jnp.where(row8 == 1, check1, 0.0))
-    fetches[6].wait()
-    par_send[...] = dot_t(parent_check, ct_up[...])[0:2]
+    par_send[...] = apply(parent_check, 1)[0:2]
+
+    def leaf_route(target, py):
+        dy, _ = leaf_task(target)
+        src = py + dy
+        valid = (target < 14) & (src >= -2) & (src <= 3)
+        row = (src + 4) // 2 - 2
+        return valid, row, (src + 4) % 2
+
+    def leaf_copies():
+        for target in range(min(nx, 14)):
+            for py in range(2):
+                valid, row, src_py = leaf_route(target, py)
+                if not valid:
+                    continue
+                copy = pltpu.make_async_remote_copy(
+                    src_ref=leaf_send.at[src_py],
+                    dst_ref=leaf_recv.at[a, py],
+                    send_sem=leaf_ssem.at[target, py],
+                    recv_sem=leaf_rsem.at[a, py],
+                    device_id=(target, wrap(b - row, ny)),
+                    device_id_type=MESH,
+                )
+                yield target, py, row, src_py, copy
+
+    def leaf_start():
+        for target, py, row, src_py, copy in leaf_copies():
+            if row:
+                copy.start()
+                continue
+
+            @pl.when(target != a)
+            def _():
+                copy.start()
+
+            @pl.when(target == a)
+            def _():
+                leaf_recv[a, py] = leaf_send[src_py]
+
+    def leaf_drain():
+        for target, py, row, src_py, copy in leaf_copies():
+            if row:
+                copy.wait_send()
+                continue
+
+            @pl.when(target != a)
+            def _():
+                copy.wait_send()
+
+    def par_copy(target):
+        to_b = wrap(b - target + nx // 2, ny)
+        copy = pltpu.make_async_remote_copy(
+            src_ref=par_send,
+            dst_ref=par_recv.at[a],
+            send_sem=par_ssem.at[target],
+            recv_sem=par_rsem.at[a],
+            device_id=(target, to_b),
+            device_id_type=MESH,
+        )
+        return (target == a) & (to_b == b), copy
+
+    def par_start(target, carry):
+        self_copy, copy = par_copy(target)
+
+        @pl.when(jnp.logical_not(self_copy))
+        def _():
+            copy.start()
+
+        @pl.when(self_copy)
+        def _():
+            par_recv[a] = par_send[...]
+
+        return carry
+
+    pl.semaphore_wait(barrier, (nx - 1) + 8 + 12 + jnp.where(a == nx // 2, nx - 1, nx))
+    lax.fori_loop(0, nx, par_start, 0)
+    leaf_start()
+    for index in range(8):
+        halo_copy(index).start()
+
+    for chunk in range(8):
+        rows = pl.ds(32 * chunk, 32)
+        total = jnp.zeros((32, 256), F32)
+        for comp in range(3):
+            diff = 0.9 * (u_ref[comp : comp + 1, :] - ut_ref[rows, comp : comp + 1])
+            tables[1 + comp, rows, :] = -2.0 * diff
+            total = total + diff * diff
+            if comp == 0:
+                for dx in (-3, -2, -1, 1, 2, 3):
+                    lines[dx + 3, rows, :] = (-2.0 * dx) * diff + float(dx * dx)
+        tables[0, rows, :] = total
 
     def source_rows(x, y, z):
         rows = []
@@ -356,65 +450,13 @@
 
         lax.fori_loop(low, low + 4 - abs(turn - 1), step, 0)
 
-    def leaf_route(target, py):
-        dy, _ = leaf_task(target)
-        src = py + dy
-        valid = (target < 14) & (src >= -2) & (src <= 3)
-        row = (src + 4) // 2 - 2
-        return valid, row, (src + 4) % 2
-
-    def leaf_copy(target, py):
-        valid, row, src_py = leaf_route(target, py)
-        to_b = lax.rem(b - row + ny, ny)
-        copy = pltpu.make_async_remote_copy(
-            src_ref=leaf_send.at[src_py],
-            dst_ref=leaf_recv.at[a, py],
-            send_sem=leaf_ssem.at[target, py],
-            recv_sem=leaf_rsem.at[a, py],
-            device_id=(target, to_b),
-            device_id_type=MESH,
-        )
-        self_copy = (target == a) & (to_b == b)
-        return valid, self_copy, src_py, copy
-
-    def leaf_start(target, carry):
-        for py in range(2):
-            valid, self_copy, src_py, copy = leaf_copy(target, py)
-
-            @pl.when(valid & jnp.logical_not(self_copy))
-            def _():
-                copy.start()
-
-            @pl.when(valid & self_copy)
-            def _():
-                leaf_recv[a, py] = leaf_send[src_py]
-
-        return carry
-
-    def par_copy(target):
-        to_b = lax.rem(b - target + nx // 2 + ny, ny)
-        copy = pltpu.make_async_remote_copy(
-            src_ref=par_send,
-            dst_ref=par_recv.at[a],
-            send_sem=par_ssem.at[target],
-            recv_sem=par_rsem.at[a],
-            device_id=(target, to_b),
-            device_id_type=MESH,
-        )
-        return (target == a) & (to_b == b), copy
-
-    def par_start(target, carry):
-        self_copy, copy = par_copy(target)
-
-        @pl.when(jnp.logical_not(self_copy))
-        def _():
-            copy.start()
-
-        @pl.when(self_copy)
-        def _():
-            par_recv[a] = par_send[...]
-
-        return carry
+    for turn in (1, 0, 2):
+        near_own(turn)
+
+    fetches[7].wait()
+    fetches[8].wait()
+    prepare(cl_down, 2)
+    prepare(ct_down, 3)
 
     for px in range(2):
         for py in range(2):
@@ -428,24 +470,14 @@
                     total = total + diff * diff
                 k_parent[box] = lax.rsqrt(total)
 
-    pl.semaphore_wait(barrier, (nx - 1) + 8 + 12 + jnp.where(a == nx // 2, nx - 1, nx))
-    lax.fori_loop(0, nx, par_start, 0)
-    lax.fori_loop(0, nx, leaf_start, 0)
-    for index in range(8):
-        halo_copy(index).start()
-
-    for turn in (1, 0, 2):
-        near_own(turn)
-
     def par_wait(source, carry):
-        from_b = lax.rem(b + a - nx // 2 + ny, ny)
-        self_copy = (source == a) & (from_b == b)
+        self_copy = (source == a) & (far_b == b)
         arrived = pltpu.make_async_remote_copy(
             src_ref=par_send,
             dst_ref=par_recv.at[source],
             send_sem=par_ssem.at[source],
             recv_sem=par_rsem.at[source],
-            device_id=(lax.rem(a + 1, nx), b),
+            device_id=(wrap(a + 1, nx), b),
             device_id_type=MESH,
         )
 
@@ -482,7 +514,7 @@
                 high, low = split(lax.rsqrt(value))
                 m_hi[first_slot + slot, rows, :] = high
                 m_lo[first_slot + slot, rows, :] = low
-        turn = lax.rem(nx + nx // 2 - index, nx)
+        turn = wrap(nx + nx // 2 - index, nx)
         p0h, p0l = split(jnp.where(keep, pltpu.roll(par_ring[0], turn, 0), 0.0))
         p1h, p1l = split(jnp.where(keep, pltpu.roll(par_ring[1], turn, 0), 0.0))
         same = bdot(jnp.concatenate([p0h, p1h, p0l, p1l], axis=0), m_hi[first_slot + 1])
@@ -512,20 +544,21 @@
 
     dy, half_z = leaf_task(a)
 
+    routes = [leaf_route(a, py) for py in range(2)]
+
     def leaf_wait(source, carry):
         for py in range(2):
-            valid, row, src_py = leaf_route(a, py)
-            self_copy = (source == a) & (row == 0)
+            valid, row, _ = routes[py]
             arrived = pltpu.make_async_remote_copy(
                 src_ref=leaf_send.at[0],
                 dst_ref=leaf_recv.at[source, py],
                 send_sem=leaf_ssem.at[source, py],
                 recv_sem=leaf_rsem.at[source, py],
-                device_id=(lax.rem(a + 1, nx), b),
+                device_id=(wrap(a + 1, nx), b),
                 device_id_type=MESH,
             )
 
-            @pl.when(valid & jnp.logical_not(self_copy))
+            @pl.when(valid & ((source != a) | (row != 0)))
             def _():
                 arrived.wait_recv()
 
@@ -625,7 +658,7 @@
         )
 
     def rs_start(step, carry):
-        rs_copy(lax.rem(a + step, nx)).start()
+        rs_copy(wrap(a + step, nx)).start()
         return carry
 
     lax.fori_loop(1, nx, rs_start, 0)
@@ -668,8 +701,27 @@
     for turn in (1, 0, 2):
         near_halo(turn)
 
+    for index in range(8):
+        halo_copy(index).wait_send()
+    leaf_drain()
+
+    def drain(target, carry):
+        own, copy = par_copy(target)
+
+        @pl.when(jnp.logical_not(own))
+        def _():
+            copy.wait_send()
+
+        @pl.when(target != a)
+        def _():
+            rs_copy(target).wait_send()
+
+        return carry
+
+    lax.fori_loop(0, nx, drain, 0)
+
     def rs_wait(step, carry):
-        source = lax.rem(a + step, nx)
+        source = wrap(a + step, nx)
         pltpu.make_async_remote_copy(
             src_ref=rs_send.at[source],
             dst_ref=rs_recv.at[source],
@@ -686,10 +738,8 @@
         for part in range(3):
             sums[part] = sums[part] + rs_recv[source, part]
 
-    fetches[7].wait()
-    fetches[8].wait()
-    leaf_local = dot_t(jnp.concatenate([sums[0], sums[1]], axis=0), cl_down[...])
-    parent_local = 0.5 * dot_t(sums[2], ct_down[...])
+    leaf_local = apply(jnp.concatenate([sums[0], sums[1]], axis=0), 2)
+    parent_local = 0.5 * apply(sums[2], 3)
     lanes = lax.broadcasted_iota(jnp.int32, (128, 128), 1)
     columns = jnp.zeros((128, 128), F32)
     for box in range(16):
@@ -708,31 +758,6 @@
                 out_ref[px, py, k : k + 1, :] = jnp.where(
                     lane128[0:1] < counts_ref[px, py, k], row, 0.0
                 )
-
-    for index in range(8):
-        halo_copy(index).wait_send()
-
-    def drain(target, carry):
-        for py in range(2):
-            valid, self_copy, _, copy = leaf_copy(target, py)
-
-            @pl.when(valid & jnp.logical_not(self_copy))
-            def _():
-                copy.wait_send()
-
-        own, copy = par_copy(target)
-
-        @pl.when(jnp.logical_not(own))
-        def _():
-            copy.wait_send()
-
-        @pl.when(target != a)
-        def _():
-            rs_copy(target).wait_send()
-
-        return carry
-
-    lax.fori_loop(0, nx, drain, 0)
 
 
 def shards(offsets, charges, counts, cl_up, cl_down, ct_up, ct_down):
@@ -781,6 +806,8 @@
             pltpu.VMEM((7, 768, 256), BF16),
             pltpu.VMEM((8, 256, 256), F32),
             pltpu.VMEM((16, 128, 128), F32),
+            pltpu.VMEM((4, 256, 256), BF16),
+            pltpu.VMEM((4, 256, 256), BF16),
             pltpu.VMEM((3, 16, 128, 32), BF16),
             pltpu.VMEM((512, 128), F32),
             pltpu.VMEM((4, 32, 512), BF16),

time: 39.7 us -> 36.5 us (0.919)
  the two profiles are of different devices: /device:TPU:27 before, /device:TPU:1 now
where the time goes in v6:
time: 36.5 us; the launch traced here: 36.2 us
  Pallas kernels  34.9 us (96%)
  local copies, waits for them, and re-layouts  1.3 us (4%)
    pallas_call x1, Pallas kernels, shards(): pl.pallas_call(functools.partial(body, nx, ny), out_shape=jax.ShapeDtypeS...  34.9 us
    unnamed x1, local copies, waits for them, and re-layouts  1.3 us

profile of v6, /device:TPU:1, one launch (start us, length us, event | category | flops | bytes accessed | tf_op | source)
XLA Modules:
  0.0 36.2 jit_solution(14844528044507405125)
XLA Ops:
  0.0 34.9 %multipole.1 = f32[2,2,4,128]{3,2,1,0:T(4,128)} custom-call(s32[2,2,4]{2,1,0:T(2,128)} %counts_hbm.1, f32[3,2,2,4,128]{4,3,2,1,0:T(4,128)} %off_hbm.1, f32[2,2,4,128]{3,2,1,0:T(4,128)} %chg_hbm.1, f32[8,256]{1,0:T(8,128)} %constant.4.clone.u_hbm, f32[256,8]{1,0:T(8,128)} %constant.5.clone.ut_hbm, f32[256,256]{1,0:T(8,128)} %cl_up_hbm.1, ...), custom_call_target="tpu_custom_call" | custom-call | tf_op jit(solution)/shard_map/multipole/pallas_call | solution.py:773
  34.9 1.3 %copy.11 = f32[2,2,4,128]{3,2,1,0:T(4,128)} copy(f32[2,2,4,128]{3,2,1,0:T(4,128)} %multipole.1) | data formatting | bytes 16384

commit v7 on v6

--- a/solution.py
+++ b/solution.py
@@ -118,37 +118,6 @@
     b = lax.axis_index("gy")
     lane128 = lax.broadcasted_iota(jnp.int32, (4, 128), 1)
 
-    barrier = pltpu.get_barrier_semaphore()
-
-    def hello(to_a, to_b):
-        pl.semaphore_signal(barrier, inc=1, device_id=(to_a, to_b), device_id_type=MESH)
-
-    def hello_row(step, carry):
-        hello(wrap(a + step, nx), b)
-        return carry
-
-    lax.fori_loop(1, nx, hello_row, 0)
-    for sx, sy in SIDES:
-        hello(wrap(a + sx, nx), wrap(b + sy, ny))
-    task_dy, _ = leaf_task(a)
-    leaf_row = jnp.where(task_dy > 0, 1, -1)
-    far_b = wrap(b + a - nx // 2, ny)
-    leaf_b = wrap(b + leaf_row, ny)
-
-    def hello_far(step, carry):
-        to_a = wrap(a + step, nx)
-
-        @pl.when((a < 14) & (task_dy != 0))
-        def _():
-            hello(to_a, leaf_b)
-
-        @pl.when((to_a != a) | (far_b != b))
-        def _():
-            hello(to_a, far_b)
-
-        return carry
-
-    lax.fori_loop(0, nx, hello_far, 0)
     fetches = [
         pltpu.make_async_copy(src, dst, in_sem.at[index])
         for index, (src, dst) in enumerate(
@@ -167,6 +136,34 @@
     ]
     for fetch in fetches:
         fetch.start()
+
+    barrier = pltpu.get_barrier_semaphore()
+
+    def hello(to_a, to_b):
+        pl.semaphore_signal(barrier, inc=1, device_id=(to_a, to_b), device_id_type=MESH)
+
+    for sx, sy in SIDES:
+        hello(wrap(a + sx, nx), wrap(b + sy, ny))
+    for step in range(1, nx):
+        hello(wrap(a + step, nx), b)
+    task_dy, _ = leaf_task(a)
+    leaf_row = jnp.where(task_dy > 0, 1, -1)
+    far_b = wrap(b + a - nx // 2, ny)
+    leaf_b = wrap(b + leaf_row, ny)
+
+    @pl.when((a < 14) & (task_dy != 0))
+    def _():
+        for to_a in range(nx):
+            hello(to_a, leaf_b)
+
+    for to_a in range(nx):
+        if to_a != nx // 2:
+            hello(to_a, far_b)
+
+    @pl.when(a != nx // 2)
+    def _():
+        hello(nx // 2, far_b)
+
     for fetch in fetches[:5]:
         fetch.wait()
 
@@ -327,23 +324,23 @@
             device_id=(target, to_b),
             device_id_type=MESH,
         )
-        return (target == a) & (to_b == b), copy
-
-    def par_start(target, carry):
-        self_copy, copy = par_copy(target)
-
-        @pl.when(jnp.logical_not(self_copy))
+        return copy
+
+    def par_start():
+        for target in range(nx):
+            if target != nx // 2:
+                par_copy(target).start()
+
+        @pl.when(a != nx // 2)
         def _():
-            copy.start()
-
-        @pl.when(self_copy)
+            par_copy(nx // 2).start()
+
+        @pl.when(a == nx // 2)
         def _():
             par_recv[a] = par_send[...]
 
-        return carry
-
     pl.semaphore_wait(barrier, (nx - 1) + 8 + 12 + jnp.where(a == nx // 2, nx - 1, nx))
-    lax.fori_loop(0, nx, par_start, 0)
+    par_start()
     leaf_start()
     for index in range(8):
         halo_copy(index).start()
@@ -657,11 +654,8 @@
             device_id_type=MESH,
         )
 
-    def rs_start(step, carry):
+    for step in range(1, nx):
         rs_copy(wrap(a + step, nx)).start()
-        return carry
-
-    lax.fori_loop(1, nx, rs_start, 0)
     rs_recv[a] = rs_send[a]
 
     for index in range(8):
@@ -706,11 +700,9 @@
     leaf_drain()
 
     def drain(target, carry):
-        own, copy = par_copy(target)
-
-        @pl.when(jnp.logical_not(own))
+        @pl.when((target != nx // 2) | (a != nx // 2))
         def _():
-            copy.wait_send()
+            par_copy(target).wait_send()
 
         @pl.when(target != a)
         def _():

time: 36.5 us -> 35.9 us (0.984)
  Pallas kernels: 34.9 us -> 34.5 us
    pallas_call x1, Pallas kernels: 34.9 us -> 34.5 us  [shards(): pl.pallas_call(functools.partial(body, nx, ny), out_shape=jax.ShapeDtypeS...]
where the time goes in v7:
time: 35.9 us; the launch traced here: 35.8 us
  Pallas kernels  34.5 us (96%)
  local copies, waits for them, and re-layouts  1.3 us (4%)
    pallas_call x1, Pallas kernels, shards(): pl.pallas_call(functools.partial(body, nx, ny), out_shape=jax.ShapeDtypeS...  34.5 us
    unnamed x1, local copies, waits for them, and re-layouts  1.3 us

profile of v7, /device:TPU:1, one launch (start us, length us, event | category | flops | bytes accessed | tf_op | source)
XLA Modules:
  0.0 35.8 jit_solution(2104098182080977581)
XLA Ops:
  0.0 34.5 %multipole.1 = f32[2,2,4,128]{3,2,1,0:T(4,128)} custom-call(s32[2,2,4]{2,1,0:T(2,128)} %counts_hbm.1, f32[3,2,2,4,128]{4,3,2,1,0:T(4,128)} %off_hbm.1, f32[2,2,4,128]{3,2,1,0:T(4,128)} %chg_hbm.1, f32[8,256]{1,0:T(8,128)} %constant.4.clone.u_hbm, f32[256,8]{1,0:T(8,128)} %constant.5.clone.ut_hbm, f32[256,256]{1,0:T(8,128)} %cl_up_hbm.1, ...), custom_call_target="tpu_custom_call" | custom-call | tf_op jit(solution)/shard_map/multipole/pallas_call | solution.py:765
  34.5 1.3 %copy.11 = f32[2,2,4,128]{3,2,1,0:T(4,128)} copy(f32[2,2,4,128]{3,2,1,0:T(4,128)} %multipole.1) | data formatting | bytes 16384
